TPU v7x, 128 devices: a whole 4x4x4 slice. The times are simulated.
128 devices in a mesh: frame: 64 (over x_hi, y, z, core), chan: 2 (over x_lo).
Axes of the slice: x: 4 (x_hi: 2, x_lo: 2; x = x_hi * 2 + x_lo), y: 4, z: 4, core: 2. Of those that a mesh axis runs over, the one named last changes fastest.
Arguments:
- clip: bfloat16 [128, 256, 1408], P('frame'), may hold values from -6 to 6
- gain: bfloat16 [1408], replicated, may hold values from 0.25 to 1.75
- w_qkv: bfloat16 [3, 1408, 1408], P(None, None, 'chan'), may hold values from -0.15625 to 0.15625
- w_out: bfloat16 [1408, 1408], P('chan'), may hold values from -0.15625 to 0.15625
- old_table: bfloat16 [1024, 1408], replicated, may hold values from -6 to 6
- target_ids: int32 [128, 256], P('frame'), may hold values from 0 to 1023
Outputs:
- d_clip: bfloat16 [128, 256, 1408], P('frame')
- d_qkv: float32 [3, 1408, 1408], P(None, 'frame', 'chan')
- d_out: float32 [1408, 1408], P('chan', 'frame')
All inputs are finite; a program needn't handle non-finite values.
Results may differ from a plain program's by a relative error of at most 0.018.
Values may be sent and summed in bfloat16 or wider, within the bound.
A program may use at most 128 MiB of HBM per device.

v0:
```python
import jax
import jax.numpy as jnp
from jax import lax
from jax.sharding import PartitionSpec as P

HEAD_DIM = 88


EPS = 1e-05


def body(clip, gain, w_qkv, w_out, old_table, target_ids):
    frames_here, patches, width = clip.shape
    cols = w_qkv.shape[2]
    heads_here = cols // HEAD_DIM
    groups = lax.axis_size("frame")
    patch_here = patches // groups
    total = frames_here * groups
    scale = HEAD_DIM ** (-0.5)
    gain_float = gain.astype(jnp.float32)
    xf = clip.astype(jnp.float32)
    row_average = jnp.mean(xf, axis=-1, keepdims=True)
    centered_input = xf - row_average
    var = jnp.mean(centered_input * centered_input, axis=-1, keepdims=True)
    inverse_deviation = lax.rsqrt(var + EPS)
    standardized_input = centered_input * inverse_deviation
    normalized_rows = (standardized_input * gain_float).astype(jnp.bfloat16)
    flat = normalized_rows.reshape(-1, width)
    qkv = jnp.einsum("td,idh->ith", flat, w_qkv, preferred_element_type=jnp.float32).astype(
        jnp.bfloat16
    )
    spread = lax.all_to_all(
        qkv.reshape(3, frames_here, groups, patch_here, cols),
        "frame",
        split_axis=2,
        concat_axis=1,
        tiled=True,
    )
    spread = spread.reshape(3, total, patch_here, heads_here, HEAD_DIM)
    query, keys, values = (spread[0], spread[1], spread[2])
    scores = jnp.einsum("fphe,gphe->phfg", query, keys, preferred_element_type=jnp.float32) * scale
    top = jnp.max(scores, axis=-1, keepdims=True)
    expo = jnp.exp(scores - top)
    probs = expo / jnp.sum(expo, axis=-1, keepdims=True)
    weights = probs.astype(jnp.bfloat16)
    attn_patch = jnp.einsum(
        "phfg,gphe->fphe", weights, values, preferred_element_type=jnp.float32
    ).astype(jnp.bfloat16)
    returned = lax.all_to_all(
        attn_patch.reshape(groups, frames_here, 1, patch_here, cols),
        "frame",
        split_axis=0,
        concat_axis=2,
        tiled=True,
    )
    attn = returned.reshape(frames_here * patches, cols)
    part = jnp.dot(attn, w_out, preferred_element_type=jnp.float32)
    branch = lax.psum(part.astype(jnp.bfloat16), "chan").astype(jnp.float32)
    y_full = xf.reshape(-1, width) + branch
    target = jnp.take(old_table, target_ids.reshape(-1), axis=0).astype(jnp.float32)
    d_y = (y_full - target).astype(jnp.bfloat16)
    d_attn = jnp.einsum("td,hd->th", d_y, w_out, preferred_element_type=jnp.float32).astype(
        jnp.bfloat16
    )
    moved = lax.all_to_all(
        d_attn.reshape(frames_here, groups, patch_here, cols),
        "frame",
        split_axis=1,
        concat_axis=0,
        tiled=True,
    )
    moved = moved.reshape(total, patch_here, heads_here, HEAD_DIM)
    dprobs = jnp.einsum("fphe,gphe->phfg", moved, values, preferred_element_type=jnp.float32)
    rowsum = jnp.sum(dprobs * probs, axis=-1, keepdims=True)
    dscore = (probs * (dprobs - rowsum) * scale).astype(jnp.bfloat16)
    dquery = jnp.einsum("phfg,gphe->fphe", dscore, keys, preferred_element_type=jnp.float32).astype(
        jnp.bfloat16
    )
    dkeys = jnp.einsum("phfg,fphe->gphe", dscore, query, preferred_element_type=jnp.float32).astype(
        jnp.bfloat16
    )
    dvalues = jnp.einsum(
        "phfg,fphe->gphe", weights, moved, preferred_element_type=jnp.float32
    ).astype(jnp.bfloat16)
    stacked = jnp.stack([dquery, dkeys, dvalues]).reshape(
        3, groups, frames_here, 1, patch_here, cols
    )
    home = lax.all_to_all(stacked, "frame", split_axis=1, concat_axis=3, tiled=True)
    grads = home.reshape(3, frames_here * patches, cols)
    d_out_part = jnp.einsum("th,td->hd", attn, d_y, preferred_element_type=jnp.float32)
    d_qkv_part = jnp.einsum("td,ith->idh", flat, grads, preferred_element_type=jnp.float32)
    d_qkv_shard, d_out_shard = (
        lax.psum_scatter(d_qkv_part, "frame", scatter_dimension=1, tiled=True),
        lax.psum_scatter(d_out_part, "frame", scatter_dimension=1, tiled=True),
    )
    d_part = jnp.einsum("ith,idh->td", grads, w_qkv, preferred_element_type=jnp.float32)
    d_norm = lax.psum(d_part.astype(jnp.bfloat16), "chan").astype(jnp.float32)
    gain_scaled = d_norm.reshape(frames_here, patches, width) * gain_float
    norm_backward_pass = inverse_deviation * (
        gain_scaled
        - jnp.mean(gain_scaled, axis=-1, keepdims=True)
        - standardized_input * jnp.mean(gain_scaled * standardized_input, axis=-1, keepdims=True)
    )
    d_clip = (
        d_y.reshape(frames_here, patches, width).astype(jnp.float32) + norm_backward_pass
    ).astype(jnp.bfloat16)
    return (d_clip, d_qkv_shard, d_out_shard)


def solution(mesh):
    return jax.shard_map(
        body,
        mesh=mesh,
        in_specs=(
            P("frame", None, None),
            P(),
            P(None, None, "chan"),
            P("chan", None),
            P(),
            P("frame", None),
        ),
        out_specs=(P("frame", None, None), P(None, "frame", "chan"), P("chan", "frame")),
        check_vma=False,
    )
```

profile of v0, /device:TPU:0, one launch (start us, length us, event | category | flops | bytes accessed | tf_op | source)
XLA Modules:
  0.0 1074.5 jit_solution(6419497599799323072)
XLA Ops:
  11.4 7.5 convert_bitcast_fusion
  18.9 4.2 copy.46
  23.1 5.2 reshape.125
  30.7 45.1 %all_to_all.60 = bf16[3,2,64,4,704]{4,3,1,0,2:T(4,128)(2,1)S(1)} all-to-all(bf16[3,2,64,4,704]{4,3,1,0,2:T(4,128)(2,1)S(1)} %copy.47), channel_id=1, replica_groups=mesh['frame'=64,'chan'=2] {'frame'}, dimensions={2} | all-to-all | bytes 4325376 | tf_op jit(solution)/shard_map/all_to_all | solution.py:32
  77.8 3.1 squeeze.11
  95.0 3.6 fusion.45
  98.5 3.2 fusion.29
  104.4 3.1 reshape.126
  107.5 21.7 %all_to_all.61 = bf16[64,2,1,4,704]{4,3,1,2,0:T(4,128)(2,1)S(1)} all-to-all(bf16[64,2,1,4,704]{4,3,1,2,0:T(4,128)(2,1)} %bitcast.96), channel_id=1, replica_groups=mesh['frame'=64,'chan'=2] {'frame'}, dimensions={0} | all-to-all | bytes 1441792 | tf_op jit(solution)/shard_map/all_to_all | solution.py:49
  132.6 4.3 convolution_convert_fusion
  140.4 48.5 %all-reduce.7.cloned.1.call-done = bf16[512,1408]{1,0:T(8,128)(2,1)} async-done(((bf16[512,1408]{1,0:T(8,128)(2,1)}), bf16[512,1408]{1,0:T(8,128)(2,1)}) %all-reduce.7.cloned.1.call-update) | async-done | bytes 1441808 | tf_op jit(solution)/shard_map/psum | solution.py:58
  198.1 25.6 %all_to_all.62 = bf16[2,64,4,704]{3,2,0,1:T(4,128)(2,1)} all-to-all(bf16[2,64,4,704]{3,2,0,1:T(4,128)(2,1)S(1)} %copy.56), channel_id=1, replica_groups=mesh['frame'=64,'chan'=2] {'frame'}, dimensions={1} | all-to-all | bytes 1441792 | tf_op jit(solution)/shard_map/all_to_all | solution.py:65
  227.7 3.6 fusion.30
  233.1 5.4 fusion.26
  238.6 5.2 fusion.23
  255.4 3.3 pad_maximum_fusion
  259.5 39.3 %all_to_all.63 = bf16[3,64,2,1,4,704]{5,4,2,3,0,1:T(4,128)(2,1)S(1)} all-to-all(bf16[3,64,2,1,4,704]{5,4,2,3,0,1:T(4,128)(2,1)S(1)} %copy.68), channel_id=1, replica_groups=mesh['frame'=64,'chan'=2] {'frame'}, dimensions={1} | all-to-all | bytes 4325376 | tf_op jit(solution)/shard_map/all_to_all | solution.py:88
  301.0 5.0 reshape.132
  306.0 8.4 fusion.3
  314.5 8.1 convolution_bitcast_fusion
  322.5 18.2 %copy.72 = f32[3,1408,704]{2,0,1:T(4,128)} copy(f32[3,1408,704]{1,2,0:T(8,128)} %convolution_bitcast_fusion) | data formatting | bytes 23789568 | tf_op jit(solution)/shard_map/td,ith->idh/transpose | solution.py:91
  341.8 3.4 fusion.47
  345.3 199.3 %fusion = f32[704,24]{0,1:T(8,128)S(1)} fusion(f32[704,1408]{0,1:T(8,128)} %fusion.47), kind=kCustom, calls=%all-reduce-scatter | all-reduce-scatter fusion | flops 1081345 | bytes 4033024
  563.3 502.7 %all-reduce.11.cloned.1.call-done = f32[3,1408,704]{2,0,1:T(4,128)} async-done(((f32[3,1408,704]{2,0,1:T(4,128)}), f32[3,1408,704]{2,0,1:T(4,128)}) %all-reduce.11.cloned.1.call-update) | async-done | bytes 11894800
  (106 shorter events, 81.8 us)
Async XLA Ops:
  7.2 130.3 %copy-start = (bf16[1024,1408]{1,0:T(8,128)(2,1)S(1)}, bf16[1024,1408]{1,0:T(8,128)(2,1)}, u32[]{:S(2)}) copy-start(bf16[1024,1408]{1,0:T(8,128)(2,1)} %param.10) | copy-start | bytes 8650756
  7.2 2.5 copy-start.15
  7.2 181.8 %all-reduce.7.cloned.1.call-start = ((), (), s32[]{:S(2)}) async-start(), calls=%async_computation.4 | async-start | bytes 2883584 | tf_op jit(solution)/shard_map/psum | solution.py:58
  7.2 1.9 copy-start.2
  132.6 4.8 copy-start.14
  137.0 419.0 %all-reduce.9.cloned.1.call-start = ((), (), s32[]{:S(2)}) async-start(), calls=%async_computation.5 | async-start | bytes 2883584 | tf_op jit(solution)/shard_map/psum | solution.py:97
  189.0 3.0 copy-start.17
  192.0 148.7 %copy-start.6 = (bf16[512,1408]{1,0:T(8,128)(2,1)}, bf16[512,1408]{1,0:T(8,128)(2,1)S(1)}, u32[]{:S(2)}) copy-start(bf16[512,1408]{1,0:T(8,128)(2,1)S(1)} %fusion.6) | copy-start | bytes 4325380
  227.7 3.6 copy-start.9
  227.7 3.6 copy-start.10
  233.1 5.4 copy-start.13
  306.0 8.4 copy-start.12
  314.4 751.7 %all-reduce.11.cloned.1.call-start = ((), (), s32[]{:S(2)}) async-start(), calls=%async_computation.6 | async-start | bytes 34603008
  345.3 207.1 %copy-start.16 = (u32[128]{0:T(128)S(1)}, u32[128]{0:T(128)}, u32[]{:S(2)}) copy-start(u32[128]{0:T(128)} %constant.34) | copy-start | bytes 1540
  544.6 6.5 collective-permute-start.5
  545.9 8.4 collective-permute-start.4
  547.2 7.1 collective-permute-start.3
  548.5 5.8 collective-permute-start.2
  549.8 4.6 collective-permute-start.1
  551.1 3.3 collective-permute-start
  555.9 1.9 copy-start.4
  559.2 1.4 copy-start.5
  559.2 1.8 copy-start.7
  560.0 507.9 %copy-start.1 = (bf16[1024,1408]{1,0:T(8,128)(2,1)S(1)}, bf16[1024,1408]{1,0:T(8,128)(2,1)}, u32[]{:S(2)}) copy-start(bf16[1024,1408]{1,0:T(8,128)(2,1)} %param.10) | copy-start | bytes 8650756
  (3 other events, 3.6 us)
Sparse Core Ops, SparseCore 0:
  137.1 51.8 all-reduce.6
  314.5 54.5 all-reduce.8
  371.7 694.3 all-reduce.10
where the time goes:
time: 1080 us; the launch traced here: 1070 us
  waiting for transfers between devices  551 us (51%)
  blocking collectives  331 us (31%)
  local copies, waits for them, and re-layouts  97.2 us (9%)
  matrix products  56.7 us (5%)
  between operations  15.6 us (1%)
  other arithmetic  14.3 us (1%)
    unnamed x10, waiting for transfers between devices  503 us
    unnamed x1, blocking collectives  199 us
    psum x1, waiting for transfers between devices, body(): branch = lax.psum(part.astype(jnp.bfloat16), 'chan').astype(jnp.float32)  48.5 us
    all_to_all x1, blocking collectives, body(): lax.all_to_all(qkv.reshape(3, frames_here, groups, patch_here, cols), 'fr...  45.1 us
    all_to_all x1, blocking collectives, body(): lax.all_to_all(stacked, 'frame', split_axis=1, concat_axis=3, tiled=True)  39.3 us
    all_to_all x1, blocking collectives, body(): lax.all_to_all(d_attn.reshape(frames_here, groups, patch_here, cols), 'fr...  25.6 us
    all_to_all x1, blocking collectives, body(): lax.all_to_all(attn_patch.reshape(groups, frames_here, 1, patch_here, col...  21.7 us
  transfers between devices with their start and end apart: 9, of which 2 were waited for; matrix products, arithmetic and copies ran while one was open for 22% of the time, Pallas kernels for 0%

commit v1 on v0

v1 whole, which is shorter than its diff:
```python
import functools

import jax
import jax.numpy as jnp
from jax import lax
from jax.experimental import pallas as pl
from jax.experimental.pallas import tpu as pltpu
from jax.sharding import PartitionSpec as P

HEAD_DIM = 88
EPS = 1e-05
XH, Y, Z, CORE = 2, 4, 4, 2
ROWS = 22
PAD = 24

f32 = jnp.float32
bf16 = jnp.bfloat16


def frame_index(xh, y, z, core):
    return ((xh * Y + y) * Z + z) * CORE + core


def coordinates():
    f = lax.axis_index("frame")
    return f // (Y * Z * CORE), (f // (Z * CORE)) % Y, (f // CORE) % Z, f % CORE


def source_row(p):
    r = p % PAD
    b = (p // PAD) % 4
    xh = (p // (PAD * 4)) % 2
    a = (p // (PAD * 8)) % 4
    core = p // (PAD * 32)
    y = a + core * (b - a)
    z = b + core * (a - b)
    return jnp.where(r < ROWS, frame_index(xh, y, z, core) * ROWS + r, -1)


def add_blocks(out, terms, count):
    def step(j, _):
        total = terms[0][j].astype(f32)
        for t in terms[1:]:
            total = total + t[j].astype(f32)
        out[j] = total.astype(out.dtype)
        return 0

    lax.fori_loop(0, count, step, 0)


def reduce_scatter_kernel(
    g, out, own, sib, summed, r1, l1, r2, l2, r3, l3, t, mr, ml,
    br1, bl1, br2, bl2, br3, bl3, u, bmr, bml, xr,
    local_sem, core_send, core_recv, a_send, a_recv, b_send, b_recv, x_send, x_recv,
):
    xh, y, z, core = coordinates()
    here = y * (1 - core) + z * core
    there = z * (1 - core) + y * core

    def ring(first, step):
        dy = step if first else 0
        dz = 0 if first else step
        ny = (y + (1 - core) * dy + core * dz + Y) % Y
        nz = (z + core * dy + (1 - core) * dz + Z) % Z
        return {"frame": frame_index(xh, ny, nz, core)}

    sibling = {"frame": frame_index(xh, y, z, 1 - core)}
    across = {"frame": frame_index(1 - xh, y, z, core)}
    barrier = pltpu.get_barrier_semaphore()
    for peer in (sibling, across, ring(True, 1), ring(True, -1), ring(False, 1), ring(False, -1)):
        pl.semaphore_signal(barrier, inc=1, device_id=peer, device_id_type=pl.DeviceIdType.MESH)
    pl.semaphore_wait(barrier, 6)

    def remote(src, dst, send, recv, peer):
        return pltpu.make_async_remote_copy(
            src_ref=src, dst_ref=dst, send_sem=send, recv_sem=recv,
            device_id=peer, device_id_type=pl.DeviceIdType.MESH,
        )

    order = ((2, 0), (2, 1), (1, 1), (3, 0), (1, 0), (3, 1), (0, 0), (0, 1))
    mine = [((here + da) % 4, h) for da, h in order]
    theirs = [((there + da) % 4, h) for da, h in order]
    swaps, loads = [], []
    for i in range(8):
        a, h = theirs[i]
        c = remote(g.at[1 - core, a, h], sib.at[i], core_send.at[i], core_recv.at[i], sibling)
        c.start()
        swaps.append(c)
        a, h = mine[i]
        c = pltpu.make_async_copy(g.at[core, a, h], own.at[i], local_sem.at[i])
        c.start()
        loads.append(c)

    def fold(i):
        loads[i].wait()
        swaps[i].wait_recv()
        add_blocks(summed.at[i], (own.at[i], sib.at[i]), 4)

    right, left = ring(True, 1), ring(True, -1)
    copies = []

    def send(src, dst, k, peer, sends, recvs):
        c = remote(src, dst, sends.at[k], recvs.at[k], peer)
        c.start()
        copies.append(c)
        return c

    fold(0)
    c1r = send(summed.at[0], r1, 0, right, a_send, a_recv)
    fold(1)
    c1l = send(summed.at[1], l1, 1, left, a_send, a_recv)
    fold(2)
    c2r = send(summed.at[2], r2, 2, right, a_send, a_recv)
    fold(3)
    c2l = send(summed.at[3], l2, 3, left, a_send, a_recv)
    fold(4)
    c1r.wait_recv()
    add_blocks(mr, (summed.at[4], r1), 4)
    c3r = send(mr, r3, 4, right, a_send, a_recv)
    fold(5)
    c1l.wait_recv()
    add_blocks(ml, (summed.at[5], l1), 4)
    c3l = send(ml, l3, 5, left, a_send, a_recv)
    fold(6)
    fold(7)
    c2l.wait_recv()
    c3r.wait_recv()
    add_blocks(t.at[0], (summed.at[6], r3, l2), 4)
    c2r.wait_recv()
    c3l.wait_recv()
    add_blocks(t.at[1], (summed.at[7], r2, l3), 4)

    right, left = ring(False, 1), ring(False, -1)
    at = lambda h, d: t.at[h, (there + d) % 4]
    d1r = send(at(0, 2), br1, 0, right, b_send, b_recv)
    d1l = send(at(1, 2), bl1, 1, left, b_send, b_recv)
    d2r = send(at(1, 1), br2, 2, right, b_send, b_recv)
    d2l = send(at(0, 3), bl2, 3, left, b_send, b_recv)
    d1r.wait_recv()
    bmr[...] = (at(0, 1)[...].astype(f32) + br1[...].astype(f32)).astype(bf16)
    d3r = send(bmr, br3, 4, right, b_send, b_recv)
    d1l.wait_recv()
    bml[...] = (at(1, 3)[...].astype(f32) + bl1[...].astype(f32)).astype(bf16)
    d3l = send(bml, bl3, 5, left, b_send, b_recv)
    d2l.wait_recv()
    d3r.wait_recv()
    u[0] = at(0, 0)[...].astype(f32) + br3[...].astype(f32) + bl2[...].astype(f32)
    d2r.wait_recv()
    d3l.wait_recv()
    u[1] = at(1, 0)[...].astype(f32) + br2[...].astype(f32) + bl3[...].astype(f32)

    e = remote(u.at[1 - xh], xr, x_send, x_recv, across)
    e.start()
    e.wait_recv()
    out[...] = u[xh] + xr[...]
    e.wait_send()
    for c in swaps:
        c.wait_send()
    for c in copies:
        c.wait_send()


def reduce_scatter(g, collective_id):
    width = g.shape[-1]
    piece = (4, PAD, width)
    block = (PAD, width)
    return pl.pallas_call(
        reduce_scatter_kernel,
        out_shape=jax.ShapeDtypeStruct(block, f32),
        in_specs=[pl.BlockSpec(memory_space=pl.ANY)],
        out_specs=pl.BlockSpec(memory_space=pltpu.VMEM),
        scratch_shapes=[
            pltpu.VMEM((8,) + piece, bf16),
            pltpu.VMEM((8,) + piece, bf16),
            pltpu.VMEM((8,) + piece, bf16),
        ]
        + [pltpu.VMEM(piece, bf16)] * 6
        + [pltpu.VMEM((2,) + piece, bf16)]
        + [pltpu.VMEM(piece, bf16)] * 2
        + [pltpu.VMEM(block, bf16)] * 6
        + [pltpu.VMEM((2,) + block, f32)]
        + [pltpu.VMEM(block, bf16)] * 2
        + [pltpu.VMEM(block, f32)]
        + [
            pltpu.SemaphoreType.DMA((8,)),
            pltpu.SemaphoreType.DMA((8,)),
            pltpu.SemaphoreType.DMA((8,)),
            pltpu.SemaphoreType.DMA((6,)),
            pltpu.SemaphoreType.DMA((6,)),
            pltpu.SemaphoreType.DMA((6,)),
            pltpu.SemaphoreType.DMA((6,)),
            pltpu.SemaphoreType.DMA,
            pltpu.SemaphoreType.DMA,
        ],
        compiler_params=pltpu.CompilerParams(
            collective_id=collective_id, has_side_effects=True, vmem_limit_bytes=48 * 2**20
        ),
        name="grad_reduce_scatter",
    )(g)


def body(clip, gain, w_qkv, w_out, old_table, target_ids):
    frames_here, patches, width = clip.shape
    cols = w_qkv.shape[2]
    heads_here = cols // HEAD_DIM
    groups = lax.axis_size("frame")
    patch_here = patches // groups
    total = frames_here * groups
    tokens = total * patch_here
    scale = HEAD_DIM ** (-0.5)
    gain_float = gain.astype(f32)
    me = lax.axis_index("frame")

    all_ids = lax.all_gather(target_ids, "frame", axis=0, tiled=True)
    ids = lax.dynamic_slice_in_dim(all_ids, me * patch_here, patch_here, axis=1)
    ids = ids.T.reshape(-1)

    moved = lax.all_to_all(
        clip.reshape(frames_here, groups, patch_here, width),
        "frame", split_axis=1, concat_axis=0, tiled=True,
    )
    x = moved.reshape(total, patch_here, width).transpose(1, 0, 2).reshape(tokens, width)

    xf = x.astype(f32)
    centered = xf - jnp.mean(xf, axis=-1, keepdims=True)
    var = jnp.mean(centered * centered, axis=-1, keepdims=True)
    rstd = lax.rsqrt(var + EPS)
    xhat = centered * rstd
    normed = (xhat * gain_float).astype(bf16)
    qkv = jnp.einsum("td,idh->ith", normed, w_qkv, preferred_element_type=f32).astype(bf16)
    heads = qkv.reshape(3, patch_here, total, heads_here, HEAD_DIM).transpose(0, 1, 3, 2, 4)
    query, keys, values = heads[0], heads[1], heads[2]
    scores = jnp.einsum("phfe,phge->phfg", query, keys, preferred_element_type=f32) * scale
    top = jnp.max(scores, axis=-1, keepdims=True)
    expo = jnp.exp(scores - top)
    probs = expo / jnp.sum(expo, axis=-1, keepdims=True)
    weights = probs.astype(bf16)
    attn = jnp.einsum("phfg,phge->phfe", weights, values, preferred_element_type=f32).astype(bf16)
    attn = attn.transpose(0, 2, 1, 3).reshape(tokens, cols)
    part = jnp.dot(attn, w_out, preferred_element_type=f32)
    branch = lax.psum(part.astype(bf16), "chan").astype(f32)
    target = jnp.take(old_table, ids, axis=0).astype(f32)
    d_y = (xf + branch - target).astype(bf16)
    d_attn = jnp.einsum("td,hd->th", d_y, w_out, preferred_element_type=f32).astype(bf16)
    d_attn = d_attn.reshape(patch_here, total, heads_here, HEAD_DIM).transpose(0, 2, 1, 3)
    dprobs = jnp.einsum("phfe,phge->phfg", d_attn, values, preferred_element_type=f32)
    rowsum = jnp.sum(dprobs * probs, axis=-1, keepdims=True)
    dscore = (probs * (dprobs - rowsum) * scale).astype(bf16)
    dq = jnp.einsum("phfg,phge->phfe", dscore, keys, preferred_element_type=f32).astype(bf16)
    dk = jnp.einsum("phfg,phfe->phge", dscore, query, preferred_element_type=f32).astype(bf16)
    dv = jnp.einsum("phfg,phfe->phge", weights, d_attn, preferred_element_type=f32).astype(bf16)
    grads = jnp.stack([dq, dk, dv]).transpose(0, 1, 3, 2, 4).reshape(3, tokens, cols)

    padded = PAD * 64
    rows = source_row(lax.broadcasted_iota(jnp.int32, (width, padded), 1))
    pick = (rows == lax.broadcasted_iota(jnp.int32, (width, padded), 0)).astype(bf16)
    normed_padded = jnp.dot(normed, pick, preferred_element_type=f32).astype(bf16)
    d_y_padded = jnp.dot(d_y, pick, preferred_element_type=f32).astype(bf16)
    g_qkv = jnp.einsum("td,ith->dih", normed_padded, grads, preferred_element_type=f32)
    g_out = jnp.einsum("td,th->dh", d_y_padded, attn, preferred_element_type=f32)
    g = jnp.concatenate([g_qkv.astype(bf16), g_out.astype(bf16)[:, None]], axis=1)
    g = g.reshape(CORE, 4, XH, 4, PAD, 4 * cols)
    reduced = reduce_scatter(g, 0)[:ROWS].reshape(ROWS, 4, cols)
    d_qkv_shard = reduced[:, :3].transpose(1, 0, 2)
    d_out_shard = reduced[:, 3].T

    d_part = jnp.einsum("ith,idh->td", grads, w_qkv, preferred_element_type=f32)
    d_norm = lax.psum(d_part.astype(bf16), "chan").astype(f32)
    gs = d_norm * gain_float
    back = rstd * (
        gs
        - jnp.mean(gs, axis=-1, keepdims=True)
        - xhat * jnp.mean(gs * xhat, axis=-1, keepdims=True)
    )
    d_clip = (d_y.astype(f32) + back).astype(bf16)
    d_clip = d_clip.reshape(patch_here, total, width).transpose(1, 0, 2)
    home = lax.all_to_all(
        d_clip.reshape(groups, frames_here, patch_here, width),
        "frame", split_axis=0, concat_axis=2, tiled=True,
    )
    return (home.reshape(frames_here, patches, width), d_qkv_shard, d_out_shard)


def solution(mesh):
    return jax.shard_map(
        body,
        mesh=mesh,
        in_specs=(
            P("frame", None, None),
            P(),
            P(None, None, "chan"),
            P("chan", None),
            P(),
            P("frame", None),
        ),
        out_specs=(P("frame", None, None), P(None, "frame", "chan"), P("chan", "frame")),
        check_vma=False,
    )
```

time: 1080 us -> 419 us (0.39)
  waiting for transfers between devices: 551 us -> 93.1 us
  blocking collectives: 331 us -> 104 us
  Pallas kernels: 0 us -> 43.8 us
  local copies, waits for them, and re-layouts: 97.2 us -> 66.2 us
  starting transfers between devices: 8.29 us -> 22.2 us
    unnamed x10 -> x2, waiting for transfers between devices: 503 us -> 0.03 us
    unnamed x1 -> x0, blocking collectives: 199 us -> none
    all_to_all x4 -> x0, blocking collectives: 132 us -> none  [the longest x1 45.1 us: body(): lax.all_to_all(qkv.reshape(3, frames_here, groups, patch_here, cols), 'fr...]
    all_gather x0 -> x1, blocking collectives: none -> 104 us  [body(): all_ids = lax.all_gather(target_ids, 'frame', axis=0, tiled=True)]
    psum x2, waiting for transfers between devices: 48.5 us -> 93 us  [the longest x1 47.2 us: body(): branch = lax.psum(part.astype(bf16), 'chan').astype(f32)]
    pallas_call x0 -> x1, Pallas kernels: none -> 43.8 us  [reduce_scatter(): pl.pallas_call(reduce_scatter_kernel, out_shape=jax.ShapeDtypeStruct(bloc...]
    all_to_all x0 -> x2, starting transfers between devices: none -> 22 us  [the longest x1 11.7 us: body(): lax.all_to_all(clip.reshape(frames_here, groups, patch_here, width), 'fra...]
    squeeze x6 -> x0, local copies, waits for them, and re-layouts: 17.2 us -> none  [body(): query, keys, values = (spread[0], spread[1], spread[2])]
  transfers between devices with their start and end apart: 9 -> 4, of which waited for: 2 -> 2; matrix products, arithmetic and copies ran while one was open for 22% -> 14% of each run, Pallas kernels for 0% -> 10%
where the time goes in v1:
time: 419 us; the launch traced here: 417 us
  blocking collectives  104 us (25%)
  waiting for transfers between devices  93.1 us (22%)
  local copies, waits for them, and re-layouts  66.2 us (16%)
  matrix products  55 us (13%)
  Pallas kernels  43.8 us (10%)
  starting transfers between devices  22.2 us (5%)
  other arithmetic  19.1 us (5%)
  between operations  14.4 us (3%)
    all_gather x1, blocking collectives, body(): all_ids = lax.all_gather(target_ids, 'frame', axis=0, tiled=True)  104 us
    psum x1, waiting for transfers between devices, body(): branch = lax.psum(part.astype(bf16), 'chan').astype(f32)  47.2 us
    psum x1, waiting for transfers between devices, body(): d_norm = lax.psum(d_part.astype(bf16), 'chan').astype(f32)  45.8 us
    pallas_call x1, Pallas kernels, reduce_scatter(): pl.pallas_call(reduce_scatter_kernel, out_shape=jax.ShapeDtypeStruct(bloc...  43.8 us
    reshape x1, local copies, waits for them, and re-layouts, body(): g = g.reshape(CORE, 4, XH, 4, PAD, 4 * cols)  15.6 us
    concatenate x1, local copies, waits for them, and re-layouts, body(): jnp.concatenate([g_qkv.astype(bf16), g_out.astype(bf16)[:, None]], axis=1)  15.2 us
    all_to_all x1, starting transfers between devices, body(): lax.all_to_all(clip.reshape(frames_here, groups, patch_here, width), 'fra...  11.7 us
    dot_general x1, matrix products, body(): jnp.einsum('td,ith->dih', normed_padded, grads, preferred_element_type=f32)  10.5 us
  transfers between devices with their start and end apart: 4, of which 2 were waited for; matrix products, arithmetic and copies ran while one was open for 14% of the time, Pallas kernels for 10%

profile of v1, /device:TPU:0, one launch (start us, length us, event | category | flops | bytes accessed | tf_op | source)
XLA Modules:
  0.0 417.3 jit_solution(1720029233187770230)
XLA Ops:
  7.2 3.0 copy.48
  11.9 11.7 %all-to-all-start = ((bf16[2,64,4,1408]{3,2,0,1:T(4,128)(2,1)}), bf16[2,64,4,1408]{3,2,0,1:T(4,128)(2,1)}, u32[]{:S(2)}, u32[]{:S(2)}) async-start(bf16[2,64,4,1408]{3,2,0,1:T(4,128)(2,1)} %copy.49), calls=%async_computation | async-start | bytes 2883584 | tf_op jit(solution)/shard_map/all_to_all | solution.py:218
  23.7 103.5 %all-gather = s32[64,2,256]{2,1,0:T(2,128)S(1)} all-gather(s32[1,2,256]{2,1,0:T(2,128)S(1)} %bitcast.166), channel_id=1, replica_groups=mesh['frame'=64,'chan'=2] {'frame'}, dimensions={0}, use_global_device_ids=true | all-gather | bytes 133120 | tf_op jit(solution)/shard_map/all_gather | solution.py:214
  133.6 4.8 %convert_bitcast_fusion = bf16[3,512,704]{1,2,0:T(8,128)(2,1)} fusion(bf16[3,1408,704]{1,2,0:T(8,128)(2,1)S(1)} %bitcast.168, bf16[512,1408]{1,0:T(8,128)(2,1)S(1)} %multiply_convert_fusion), kind=kOutput, calls=%fused_computation.62 | convolution fusion | flops 3046146048 | bytes 9551872 | tf_op jit(solution)/shard_map/td,idh->ith/dot_general | solution.py:230
  138.4 4.8 %reshape.130 = bf16[3,4,128,8,88]{2,1,4,3,0:T(4,128)(2,1)} reshape(bf16[3,512,704]{1,2,0:T(8,128)(2,1)} %convert_bitcast_fusion) | data formatting | bytes 4325376 | tf_op jit(solution)/shard_map/reshape | solution.py:231
  143.2 3.3 copy.95
  146.5 3.5 fusion.86
  156.7 2.9 gather_fusion
  159.8 47.2 %all-reduce.3.cloned.1.call-done = bf16[512,1408]{1,0:T(8,128)(2,1)} async-done(((bf16[512,1408]{1,0:T(8,128)(2,1)}), bf16[512,1408]{1,0:T(8,128)(2,1)}) %all-reduce.3.cloned.1.call-update) | async-done | bytes 1441808 | tf_op jit(solution)/shard_map/psum | solution.py:241
  207.0 3.4 fusion.19
  211.9 3.4 fusion.48
  217.1 5.2 %fusion.44 = bf16[1,4,8,128,88]{3,4,2,1,0:T(8,128)(2,1)} fusion(f32[4,8,128,128]{2,3,1,0:T(8,128)} %fusion.55, bf16[3,4,8,128,88]{3,4,2,1,0:T(8,128)(2,1)S(1)} %bitcast.157, f32[4,8,128,128]{2,3,1,0:T(8,128)} %get-tuple-element.11, f32[4,8,128]{2,1,0:T(8,128)S(1)} %get-tuple-element.10), kind=kOutput, calls=%fused_computation.79 | convolution fusion | flops 96309376 | bytes 9863168 | tf_op jit(solution)/shard_map/phfg,phge->phfe/dot_general | solution.py:249
  222.3 5.2 %fusion.41 = bf16[1,4,8,128,88]{3,4,2,1,0:T(8,128)(2,1)} fusion(f32[4,8,128,128]{2,3,1,0:T(8,128)} %fusion.55, bf16[3,4,8,128,88]{3,4,2,1,0:T(8,128)(2,1)S(1)} %bitcast.158, f32[4,8,128,128]{2,3,1,0:T(8,128)} %get-tuple-element.11, f32[4,8,128]{2,1,0:T(8,128)S(1)} %get-tuple-element.10), kind=kOutput, calls=%fused_computation.78 | convolution fusion | flops 96309376 | bytes 9863168 | tf_op jit(solution)/shard_map/phfg,phfe->phge/dot_general | solution.py:250
  229.1 3.0 copy.59
  232.2 3.8 reshape.135
  236.0 8.4 %fusion.15 = bf16[512,1408]{1,0:T(8,128)(2,1)} fusion(bf16[3,512,704]{1,2,0:T(8,128)(2,1)S(1)} %reshape.135, bf16[3,1408,704]{1,2,0:T(8,128)(2,1)} %param.8), kind=kOutput, calls=%fused_computation.40 | convolution fusion | flops 3045785600 | bytes 9551872 | tf_op jit(solution)/shard_map/ith,idh->td/dot_general | solution.py:267
  244.4 10.5 %convolution_convert_fusion = bf16[1536,3,704]{0,2,1:T(8,128)(2,1)} fusion(bf16[3,512,704]{1,2,0:T(8,128)(2,1)} %copy-done.9, bf16[512,1408]{1,0:T(8,128)(2,1)} %copy-done.10, s32[1536]{0:T(1024)S(1)} %get-tuple-element.14, s32[1536]{0:T(1024)S(1)} %get-tuple-element.24, s32[1536]{0:T(1024)S(1)} %get-tuple-element.15, s32[1536]{0:T(1024)S(1)} %get-tuple-element.25, ...), kind=kOutput, calls=%fused_computation.37 | convolution fusion | flops 5659459584 | bytes 10161664 | tf_op jit(solution)/shard_map/td,ith->dih/dot_general | solution.py:259
  254.9 45.8 %all-reduce.5.cloned.1.call-done = bf16[512,1408]{1,0:T(8,128)(2,1)} async-done(((bf16[512,1408]{1,0:T(8,128)(2,1)}), bf16[512,1408]{1,0:T(8,128)(2,1)}) %all-reduce.5.cloned.1.call-update) | async-done | bytes 1441808 | tf_op jit(solution)/shard_map/psum | solution.py:268
  306.5 10.2 %all-to-all-start.1 = ((bf16[64,2,4,1408]{3,2,1,0:T(4,128)(2,1)}), bf16[64,2,4,1408]{3,2,1,0:T(4,128)(2,1)}, u32[]{:S(2)}, u32[]{:S(2)}) async-start(bf16[64,2,4,1408]{3,2,1,0:T(4,128)(2,1)} %bitcast.31), calls=%async_computation.1 | async-start | bytes 2883584 | tf_op jit(solution)/shard_map/all_to_all | solution.py:277
  316.7 5.9 %fusion.16 = bf16[1536,1,704]{0,2,1:T(8,128)(2,1)} fusion(bf16[512,1408]{1,0:T(8,128)(2,1)S(1)} %copy-done.6, bf16[88,8,4,128]{3,2,1,0:T(4,128)(2,1)S(1)} %bitcast.161, s32[1536]{0:T(1024)S(1)} %get-tuple-element.14, s32[1536]{0:T(1024)S(1)} %get-tuple-element.24, s32[1536]{0:T(1024)S(1)} %get-tuple-element.15, s32[1536]{0:T(1024)S(1)} %get-tuple-element.25, ...), kind=kOutput, calls=%fused_computation.44 | convolution fusion | flops 3442704384 | bytes 4394496 | tf_op jit(solution)/shard_map/td,th->dh/dot_general | solution.py:260
  322.6 7.6 %pad_maximum_fusion = bf16[1536,4,704]{0,2,1:T(8,128)(2,1)} fusion(bf16[1536,1,704]{0,2,1:T(8,128)(2,1)} %fusion.16, bf16[1536,3,704]{0,2,1:T(8,128)(2,1)} %convolution_convert_fusion), kind=kLoop, calls=%fused_computation.36 | loop fusion | flops 4325376 | bytes 17301504 | tf_op jit(solution)/shard_map/concatenate | solution.py:261
  330.3 15.2 %copy.62 = bf16[1536,4,704]{2,1,0:T(4,128)(2,1)} copy(bf16[1536,4,704]{0,2,1:T(8,128)(2,1)} %pad_maximum_fusion) | data formatting | bytes 17301504 | tf_op jit(solution)/shard_map/concatenate | solution.py:261
  345.5 15.6 %reshape.139.g = bf16[2,4,2,4,24,2816]{5,4,3,2,1,0:T(8,128)(2,1)} reshape(bf16[1536,4,704]{2,1,0:T(4,128)(2,1)} %copy.62) | data formatting | bytes 17301504 | tf_op jit(solution)/shard_map/reshape | solution.py:262
  361.1 43.8 %grad_reduce_scatter.1 = f32[24,2816]{1,0:T(8,128)S(1)} custom-call(bf16[2,4,2,4,24,2816]{5,4,3,2,1,0:T(8,128)(2,1)} %reshape.139.g), custom_call_target="tpu_custom_call" | custom-call | tf_op jit(solution)/shard_map/grad_reduce_scatter/pallas_call | solution.py:167
  (87 shorter events, 30.9 us)
Async XLA Ops:
  7.2 149.6 %copy-start = (bf16[1024,1408]{1,0:T(8,128)(2,1)S(1)}, bf16[1024,1408]{1,0:T(8,128)(2,1)}, u32[]{:S(2)}) copy-start(bf16[1024,1408]{1,0:T(8,128)(2,1)} %param.10) | copy-start | bytes 8650756
  10.2 13.5 %copy-start.14 = (bf16[1408]{0:T(1024)(128)(2,1)S(1)}, bf16[1408]{0:T(1024)(128)(2,1)}, u32[]{:S(2)}) copy-start(bf16[1408]{0:T(1024)(128)(2,1)} %param.7) | copy-start | bytes 8452
  10.2 13.5 %copy-start.15 = (s32[2,256]{1,0:T(2,128)S(1)}, s32[2,256]{1,0:T(2,128)}, u32[]{:S(2)}) copy-start(s32[2,256]{1,0:T(2,128)} %param.11) | copy-start | bytes 6148
  11.9 115.6 %all-to-all-start = ((bf16[2,64,4,1408]{3,2,0,1:T(4,128)(2,1)}), bf16[2,64,4,1408]{3,2,0,1:T(4,128)(2,1)}, u32[]{:S(2)}, u32[]{:S(2)}) async-start(bf16[2,64,4,1408]{3,2,0,1:T(4,128)(2,1)} %copy.49), calls=%async_computation | async-start | bytes 2883584 | tf_op jit(solution)/shard_map/all_to_all | solution.py:218
  23.6 183.4 %all-reduce.3.cloned.1.call-start = ((), (), s32[]{:S(2)}) async-start(), calls=%async_computation.2 | async-start | bytes 2883584 | tf_op jit(solution)/shard_map/psum | solution.py:241
  129.2 3.7 slice-start
  129.5 4.1 slice-start.1
  129.7 1.6 copy-start.2
  131.8 1.2 copy-start.10
  150.1 3.9 copy-start.16
  153.0 0.9 copy-start.11
  156.5 144.2 %all-reduce.5.cloned.1.call-start = ((), (), s32[]{:S(2)}) async-start(), calls=%async_computation.3 | async-start | bytes 2883584 | tf_op jit(solution)/shard_map/psum | solution.py:268
  207.0 3.4 copy-start.17
  210.4 1.3 copy-start.4
  211.9 3.4 copy-start.8
  222.3 5.2 %copy-start.13 = (bf16[1,4,8,128,88]{3,4,2,1,0:T(8,128)(2,1)S(1)}, bf16[1,4,8,128,88]{3,4,2,1,0:T(8,128)(2,1)}, u32[]{:S(2)}) copy-start(bf16[1,4,8,128,88]{3,4,2,1,0:T(8,128)(2,1)} %fusion.48) | copy-start | bytes 2162692
  236.0 8.4 %copy-start.9 = (bf16[3,512,704]{1,2,0:T(8,128)(2,1)}, bf16[3,512,704]{1,2,0:T(8,128)(2,1)S(1)}, u32[]{:S(2)}) copy-start(bf16[3,512,704]{1,2,0:T(8,128)(2,1)S(1)} %reshape.135) | copy-start | bytes 6488068
  244.4 56.3 %copy-start.3 = (f32[128,4,1408]{2,0,1:T(8,128)S(1)}, f32[128,4,1408]{2,0,1:T(8,128)}, u32[]{:S(2)}) copy-start(f32[128,4,1408]{2,0,1:T(8,128)} %copy-done.2) | copy-start | bytes 8650756
  300.7 2.4 copy-start.5
  300.7 2.4 copy-start.7
  304.2 12.5 %copy-start.6 = (bf16[512,1408]{1,0:T(8,128)(2,1)S(1)}, bf16[512,1408]{1,0:T(8,128)(2,1)}, u32[]{:S(2)}) copy-start(bf16[512,1408]{1,0:T(8,128)(2,1)} %copy-done.4) | copy-start | bytes 4325380
  304.2 12.5 %copy-start.12 = (bf16[4,128,8,88]{1,0,3,2:T(4,128)(2,1)S(1)}, bf16[4,128,8,88]{1,0,3,2:T(4,128)(2,1)}, u32[]{:S(2)}) copy-start(bf16[4,128,8,88]{1,0,3,2:T(4,128)(2,1)} %copy-done.11) | copy-start | bytes 2162692
  306.5 100.1 %all-to-all-start.1 = ((bf16[64,2,4,1408]{3,2,1,0:T(4,128)(2,1)}), bf16[64,2,4,1408]{3,2,1,0:T(4,128)(2,1)}, u32[]{:S(2)}, u32[]{:S(2)}) async-start(bf16[64,2,4,1408]{3,2,1,0:T(4,128)(2,1)} %bitcast.31), calls=%async_computation.1 | async-start | bytes 2883584 | tf_op jit(solution)/shard_map/all_to_all | solution.py:277
  406.6 3.9 copy-start.1
Sparse Core Ops, SparseCore 0:
  156.6 50.3 all-reduce.2
  244.5 56.1 all-reduce.4

commit v2 on v1

v2 whole, which is shorter than its diff:
```python
import functools

import jax
import jax.numpy as jnp
from jax import lax
from jax.experimental import pallas as pl
from jax.experimental.pallas import tpu as pltpu
from jax.sharding import PartitionSpec as P

HEAD_DIM = 88
EPS = 1e-05
XH, Y, Z, CORE = 2, 4, 4, 2
FRAME = XH * Y * Z * CORE
ROWS = 22
PAD = 24

f32 = jnp.float32
bf16 = jnp.bfloat16


def frame_index(xh, y, z, core):
    return ((xh * Y + y) * Z + z) * CORE + core


def coordinates():
    f = lax.axis_index("frame")
    return f // (Y * Z * CORE), (f // (Z * CORE)) % Y, (f // CORE) % Z, f % CORE


def all_peer(k):
    f = lax.axis_index("frame")
    chan = lax.axis_index("chan")
    p = (f + k) % FRAME
    far = (p // (FRAME // 2) + f // (FRAME // 2)) % 2
    return p, {"frame": p, "chan": (chan + far) % 2}


def greet_all(extra):
    barrier = pltpu.get_barrier_semaphore()

    def greet(k, _):
        pl.semaphore_signal(
            barrier, inc=1, device_id=all_peer(k)[1], device_id_type=pl.DeviceIdType.MESH
        )
        return 0

    lax.fori_loop(1, FRAME, greet, 0)
    pl.semaphore_signal(barrier, inc=1, device_id=extra, device_id_type=pl.DeviceIdType.MESH)
    pl.semaphore_wait(barrier, FRAME)


def all_copy(src, dst, sends, recvs, k):
    p, peer = all_peer(k)
    return pltpu.make_async_remote_copy(
        src_ref=src.at[p], dst_ref=dst.at[lax.axis_index("frame")],
        send_sem=sends.at[k], recv_sem=recvs.at[k],
        device_id=peer, device_id_type=pl.DeviceIdType.MESH,
    )


def start_all(src, dst, sends, recvs, own_sem):
    def start(k, _):
        all_copy(src, dst, sends, recvs, k).start()
        return 0

    lax.fori_loop(1, FRAME, start, 0)
    f = lax.axis_index("frame")
    pltpu.make_async_copy(src.at[f], dst.at[f], own_sem).start()


def wait_all(src, dst, sends, recvs, own_sem):
    f = lax.axis_index("frame")
    pltpu.make_async_copy(src.at[f], dst.at[f], own_sem).wait()

    def wait(k, _):
        all_copy(src, dst, sends, recvs, k).wait_recv()
        return 0

    lax.fori_loop(1, FRAME, wait, 0)

    def drain(k, _):
        all_copy(src, dst, sends, recvs, k).wait_send()
        return 0

    lax.fori_loop(1, FRAME, drain, 0)


def gather_kernel(src, w, dst, w_other, sends, recvs, own_sem, w_send, w_recv):
    xh, y, z, core = coordinates()
    chan = lax.axis_index("chan")
    partner = {"chan": 1 - chan}
    sibling = {"frame": frame_index(xh, y, z, 1 - core)}
    greet_all(partner)

    def remote(s, d, k, peer):
        return pltpu.make_async_remote_copy(
            src_ref=s, dst_ref=d, send_sem=w_send.at[k], recv_sem=w_recv.at[k],
            device_id=peer, device_id_type=pl.DeviceIdType.MESH,
        )

    first = remote(w.at[core], w_other.at[core], 0, partner)
    first.start()
    start_all(src, dst, sends, recvs, own_sem)
    first.wait_recv()
    second = remote(w_other.at[core], w_other.at[core], 1, sibling)
    second.start()
    second.wait_recv()
    first.wait_send()
    second.wait_send()
    wait_all(src, dst, sends, recvs, own_sem)


def gather_clip(src, w):
    any_spec = pl.BlockSpec(memory_space=pl.ANY)
    return pl.pallas_call(
        gather_kernel,
        out_shape=[
            jax.ShapeDtypeStruct(src.shape, src.dtype),
            jax.ShapeDtypeStruct(w.shape, w.dtype),
        ],
        in_specs=[pl.BlockSpec(memory_space=pltpu.VMEM), any_spec],
        out_specs=[pl.BlockSpec(memory_space=pltpu.VMEM), any_spec],
        scratch_shapes=[
            pltpu.SemaphoreType.DMA((FRAME,)),
            pltpu.SemaphoreType.DMA((FRAME,)),
            pltpu.SemaphoreType.DMA,
            pltpu.SemaphoreType.DMA((2,)),
            pltpu.SemaphoreType.DMA((2,)),
        ],
        compiler_params=pltpu.CompilerParams(
            collective_id=1, has_side_effects=True, vmem_limit_bytes=32 * 2**20
        ),
        name="gather_clip",
    )(src, w)


def dot(a, b):
    return jnp.dot(a, b, preferred_element_type=f32)


def dot_nt(a, b):
    return lax.dot_general(a, b, (((1,), (1,)), ((), ())), preferred_element_type=f32)


def dot_tn(a, b):
    return lax.dot_general(a, b, (((0,), (0,)), ((), ())), preferred_element_type=f32)


def iota(shape, dim):
    return lax.broadcasted_iota(jnp.int32, shape, dim)


def norm_terms(x):
    centered = x - jnp.mean(x, axis=-1, keepdims=True)
    rstd = lax.rsqrt(jnp.mean(centered * centered, axis=-1, keepdims=True) + EPS)
    return centered * rstd, rstd


def sublayer_kernel(
    r, gain, w_qkv, w_out, w_other, table, home, g,
    x_s, ids_s, n_s, q_s, k_s, v_s, o_s, oo_s, p_s, dy_s, do_s, dq_s, dk_s, dv_s, dn_s, dno_s, d_s,
    o_send, o_recv, dn_send, dn_recv,
):
    width = x_s.shape[1]
    cols = q_s.shape[1]
    n_heads = cols // HEAD_DIM
    frames = 128
    tokens = x_s.shape[0]
    patches = tokens // frames
    scale = HEAD_DIM ** (-0.5)
    partner = {"chan": 1 - lax.axis_index("chan")}
    barrier = pltpu.get_barrier_semaphore()
    pl.semaphore_signal(barrier, inc=1, device_id=partner, device_id_type=pl.DeviceIdType.MESH)
    pl.semaphore_wait(barrier, 1)

    def rows(p):
        return pl.ds(pl.multiple_of(p * frames, frames), frames)

    def swap(src, dst, sends, recvs, p):
        return pltpu.make_async_remote_copy(
            src_ref=src.at[rows(p)], dst_ref=dst.at[rows(p)],
            send_sem=sends.at[p], recv_sem=recvs.at[p],
            device_id=partner, device_id_type=pl.DeviceIdType.MESH,
        )

    def head(ref, p, h):
        return ref[rows(p), h * HEAD_DIM : (h + 1) * HEAD_DIM]

    def forward(p, _):
        t = iota((frames, tokens), 0)
        pick = (iota((frames, tokens), 1) == (t // 2) * 8 + 2 * p + t % 2).astype(bf16)
        moved = dot(pick, r[...])
        x = moved[:, :width]
        x_s[rows(p), :] = x.astype(bf16)
        ids_s[rows(p), :] = moved[:, width:]
        xhat, _ = norm_terms(x)
        normed = (xhat * gain[...].astype(f32)).astype(bf16)
        n_s[rows(p), :] = normed
        q_s[rows(p), :] = dot(normed, w_qkv[0]).astype(bf16)
        k_s[rows(p), :] = dot(normed, w_qkv[1]).astype(bf16)
        v_s[rows(p), :] = dot(normed, w_qkv[2]).astype(bf16)
        for h in range(n_heads):
            scores = dot_nt(head(q_s, p, h), head(k_s, p, h)) * scale
            expo = jnp.exp(scores - jnp.max(scores, axis=-1, keepdims=True))
            probs = expo / jnp.sum(expo, axis=-1, keepdims=True)
            p_s[p * n_heads + h] = probs
            o_s[rows(p), h * HEAD_DIM : (h + 1) * HEAD_DIM] = dot(
                probs.astype(bf16), head(v_s, p, h)
            ).astype(bf16)
        swap(o_s, oo_s, o_send, o_recv, p).start()
        return 0

    lax.fori_loop(0, patches, forward, 0)

    def backward(p, _):
        hi_lo = ids_s[rows(p), :]
        ids = hi_lo[:, 0:1] * 32.0 + hi_lo[:, 1:2]
        n_old = table.shape[0]
        pick = (iota((frames, n_old), 1).astype(f32) == ids).astype(bf16)
        target = dot(pick, table[...])
        swap(o_s, oo_s, o_send, o_recv, p).wait_recv()
        branch = dot(o_s[rows(p), :], w_out[...]) + dot(oo_s[rows(p), :], w_other[...])
        d_y = (x_s[rows(p), :].astype(f32) + branch - target).astype(bf16)
        dy_s[rows(p), :] = d_y
        do_s[rows(p), :] = dot_nt(d_y, w_out[...]).astype(bf16)
        for h in range(n_heads):
            here = slice(h * HEAD_DIM, (h + 1) * HEAD_DIM)
            probs = p_s[p * n_heads + h]
            d_o = head(do_s, p, h)
            dprobs = dot_nt(d_o, head(v_s, p, h))
            rowsum = jnp.sum(dprobs * probs, axis=-1, keepdims=True)
            ds = (probs * (dprobs - rowsum) * scale).astype(bf16)
            dq_s[rows(p), here] = dot(ds, head(k_s, p, h)).astype(bf16)
            dk_s[rows(p), here] = dot_tn(ds, head(q_s, p, h)).astype(bf16)
            dv_s[rows(p), here] = dot_tn(probs.astype(bf16), d_o).astype(bf16)
        dn = dot_nt(dq_s[rows(p), :], w_qkv[0])
        dn = dn + dot_nt(dk_s[rows(p), :], w_qkv[1])
        dn = dn + dot_nt(dv_s[rows(p), :], w_qkv[2])
        dn_s[rows(p), :] = dn.astype(bf16)
        swap(dn_s, dno_s, dn_send, dn_recv, p).start()
        return 0

    lax.fori_loop(0, patches, backward, 0)

    block = 8 * ROWS
    window = 384

    def weight_grads(k, _):
        start = jnp.minimum(k * block // 128, (width - window) // 128) * 128
        lanes = pl.ds(pl.multiple_of(start, 128), window)
        shape = (8 * PAD, window)
        at = iota(shape, 0)
        wanted = jnp.where(at % PAD < ROWS, k * block + (at // PAD) * ROWS + at % PAD - start, -1)
        pick = (iota(shape, 1) == wanted).astype(bf16)
        normed_t = dot_nt(pick, n_s[:, lanes]).astype(bf16)
        d_y_t = dot_nt(pick, dy_s[:, lanes]).astype(bf16)
        xh, y = k // Y, k % Y
        for i, (left, right) in enumerate(
            ((normed_t, dq_s), (normed_t, dk_s), (normed_t, dv_s), (d_y_t, o_s))
        ):
            part = dot(left, right[...]).astype(bf16)
            for j in range(8):
                z, core = j // 2, j % 2
                a, b = (y, z) if core == 0 else (z, y)
                g[core, a, xh, b, :, i * cols : (i + 1) * cols] = part[j * PAD : (j + 1) * PAD]
        return 0

    lax.fori_loop(0, width // block, weight_grads, 0)

    def finish(p, _):
        swap(dn_s, dno_s, dn_send, dn_recv, p).wait_recv()
        dn = dn_s[rows(p), :].astype(f32) + dno_s[rows(p), :].astype(f32)
        xhat, rstd = norm_terms(x_s[rows(p), :].astype(f32))
        gs = dn * gain[...].astype(f32)
        back = rstd * (
            gs
            - jnp.mean(gs, axis=-1, keepdims=True)
            - xhat * jnp.mean(gs * xhat, axis=-1, keepdims=True)
        )
        d_s[rows(p), :] = (dy_s[rows(p), :].astype(f32) + back).astype(bf16)
        return 0

    lax.fori_loop(0, patches, finish, 0)

    def to_home(j, _):
        t = iota((frames, tokens), 0) + j * frames
        source = (t % 8 // 2) * frames + 2 * (t // 8) + t % 2
        pick = (iota((frames, tokens), 1) == source).astype(bf16)
        moved = dot(pick, d_s[...])
        home[pl.ds(j * (frames // 8), frames // 8)] = moved.reshape(
            frames // 8, 8, width
        ).astype(bf16)
        return 0

    lax.fori_loop(0, patches, to_home, 0)

    def drain(p, _):
        swap(o_s, oo_s, o_send, o_recv, p).wait_send()
        swap(dn_s, dno_s, dn_send, dn_recv, p).wait_send()
        return 0

    lax.fori_loop(0, patches, drain, 0)


def sublayer(r, gain, w_qkv, w_out, w_other, table):
    tokens = r.shape[0]
    width, cols = w_qkv.shape[1:]
    patches = tokens // 128
    vmem = pl.BlockSpec(memory_space=pltpu.VMEM)
    wide = pltpu.VMEM((tokens, width), bf16)
    narrow = pltpu.VMEM((tokens, cols), bf16)
    return pl.pallas_call(
        sublayer_kernel,
        out_shape=[
            jax.ShapeDtypeStruct((FRAME, 8, width), bf16),
            jax.ShapeDtypeStruct((CORE, 4, XH, 4, PAD, 4 * cols), bf16),
        ],
        in_specs=[vmem] * 6,
        out_specs=[vmem] * 2,
        scratch_shapes=[
            wide,
            pltpu.VMEM((tokens, r.shape[1] - width), f32),
            wide,
            narrow, narrow, narrow, narrow, narrow,
            pltpu.VMEM((patches * cols // HEAD_DIM, 128, 128), f32),
            wide,
            narrow, narrow, narrow, narrow,
            wide, wide, wide,
        ]
        + [pltpu.SemaphoreType.DMA((patches,))] * 4,
        compiler_params=pltpu.CompilerParams(
            collective_id=2, has_side_effects=True, vmem_limit_bytes=60 * 2**20
        ),
        name="sublayer",
    )(r, gain, w_qkv, w_out, w_other, table)


def add_blocks(out, terms, count):
    def step(j, _):
        total = terms[0][j].astype(f32)
        for t in terms[1:]:
            total = total + t[j].astype(f32)
        out[j] = total.astype(out.dtype)
        return 0

    lax.fori_loop(0, count, step, 0)


def reduce_scatter_kernel(
    g, d_send, out, d_recv, own, sib, summed, r1, l1, r2, l2, r3, l3, t, mr, ml,
    br1, bl1, br2, bl2, br3, bl3, u, bmr, bml, xr,
    local_sem, core_send, core_recv, a_send, a_recv, b_send, b_recv, x_send, x_recv, d_sems, e_sems, f_sem,
):
    xh, y, z, core = coordinates()
    chan = lax.axis_index("chan")
    here = y * (1 - core) + z * core
    there = z * (1 - core) + y * core

    def ring(first, step):
        dy = step if first else 0
        dz = 0 if first else step
        ny = (y + (1 - core) * dy + core * dz + Y) % Y
        nz = (z + core * dy + (1 - core) * dz + Z) % Z
        return {"frame": frame_index(xh, ny, nz, core)}

    sibling = {"frame": frame_index(xh, y, z, 1 - core)}
    across = {"frame": frame_index(1 - xh, y, z, core)}
    greet_all(across)

    def remote(src, dst, send, recv, peer):
        return pltpu.make_async_remote_copy(
            src_ref=src, dst_ref=dst, send_sem=send, recv_sem=recv,
            device_id=peer, device_id_type=pl.DeviceIdType.MESH,
        )

    start_all(d_send, d_recv, d_sems, e_sems, f_sem)

    order = ((2, 0), (2, 1), (1, 1), (3, 0), (1, 0), (3, 1), (0, 0), (0, 1))
    mine = [((here + da) % 4, h) for da, h in order]
    theirs = [((there + da) % 4, h) for da, h in order]
    swaps, loads = [], []
    for i in range(8):
        a, h = theirs[i]
        c = remote(g.at[1 - core, a, h], sib.at[i], core_send.at[i], core_recv.at[i], sibling)
        c.start()
        swaps.append(c)
        a, h = mine[i]
        c = pltpu.make_async_copy(g.at[core, a, h], own.at[i], local_sem.at[i])
        c.start()
        loads.append(c)

    def fold(i):
        loads[i].wait()
        swaps[i].wait_recv()
        add_blocks(summed.at[i], (own.at[i], sib.at[i]), 4)

    right, left = ring(True, 1), ring(True, -1)
    copies = []

    def send(src, dst, k, peer, sends, recvs):
        c = remote(src, dst, sends.at[k], recvs.at[k], peer)
        c.start()
        copies.append(c)
        return c

    fold(0)
    c1r = send(summed.at[0], r1, 0, right, a_send, a_recv)
    fold(1)
    c1l = send(summed.at[1], l1, 1, left, a_send, a_recv)
    fold(2)
    c2r = send(summed.at[2], r2, 2, right, a_send, a_recv)
    fold(3)
    c2l = send(summed.at[3], l2, 3, left, a_send, a_recv)
    fold(4)
    c1r.wait_recv()
    add_blocks(mr, (summed.at[4], r1), 4)
    c3r = send(mr, r3, 4, right, a_send, a_recv)
    fold(5)
    c1l.wait_recv()
    add_blocks(ml, (summed.at[5], l1), 4)
    c3l = send(ml, l3, 5, left, a_send, a_recv)
    fold(6)
    fold(7)
    c2l.wait_recv()
    c3r.wait_recv()
    add_blocks(t.at[0], (summed.at[6], r3, l2), 4)
    c2r.wait_recv()
    c3l.wait_recv()
    add_blocks(t.at[1], (summed.at[7], r2, l3), 4)

    right, left = ring(False, 1), ring(False, -1)
    at = lambda h, d: t.at[h, (there + d) % 4]
    d1r = send(at(0, 2), br1, 0, right, b_send, b_recv)
    d1l = send(at(1, 2), bl1, 1, left, b_send, b_recv)
    d2r = send(at(1, 1), br2, 2, right, b_send, b_recv)
    d2l = send(at(0, 3), bl2, 3, left, b_send, b_recv)
    d1r.wait_recv()
    bmr[...] = (at(0, 1)[...].astype(f32) + br1[...].astype(f32)).astype(bf16)
    d3r = send(bmr, br3, 4, right, b_send, b_recv)
    d1l.wait_recv()
    bml[...] = (at(1, 3)[...].astype(f32) + bl1[...].astype(f32)).astype(bf16)
    d3l = send(bml, bl3, 5, left, b_send, b_recv)
    d2l.wait_recv()
    d3r.wait_recv()
    u[0] = at(0, 0)[...].astype(f32) + br3[...].astype(f32) + bl2[...].astype(f32)
    d2r.wait_recv()
    d3l.wait_recv()
    u[1] = at(1, 0)[...].astype(f32) + br2[...].astype(f32) + bl3[...].astype(f32)

    e = remote(u.at[1 - xh], xr, x_send, x_recv, across)
    e.start()
    e.wait_recv()
    out[...] = u[xh] + xr[...]
    e.wait_send()
    for c in swaps:
        c.wait_send()
    for c in copies:
        c.wait_send()
    wait_all(d_send, d_recv, d_sems, e_sems, f_sem)


def reduce_scatter(g, home):
    width = g.shape[-1]
    piece = (4, PAD, width)
    block = (PAD, width)
    return pl.pallas_call(
        reduce_scatter_kernel,
        out_shape=[
            jax.ShapeDtypeStruct(block, f32),
            jax.ShapeDtypeStruct(home.shape, home.dtype),
        ],
        in_specs=[pl.BlockSpec(memory_space=pl.ANY), pl.BlockSpec(memory_space=pltpu.VMEM)],
        out_specs=[pl.BlockSpec(memory_space=pltpu.VMEM)] * 2,
        scratch_shapes=[
            pltpu.VMEM((8,) + piece, bf16),
            pltpu.VMEM((8,) + piece, bf16),
            pltpu.VMEM((8,) + piece, bf16),
        ]
        + [pltpu.VMEM(piece, bf16)] * 6
        + [pltpu.VMEM((2,) + piece, bf16)]
        + [pltpu.VMEM(piece, bf16)] * 2
        + [pltpu.VMEM(block, bf16)] * 6
        + [pltpu.VMEM((2,) + block, f32)]
        + [pltpu.VMEM(block, bf16)] * 2
        + [pltpu.VMEM(block, f32)]
        + [
            pltpu.SemaphoreType.DMA((8,)),
            pltpu.SemaphoreType.DMA((8,)),
            pltpu.SemaphoreType.DMA((8,)),
            pltpu.SemaphoreType.DMA((6,)),
            pltpu.SemaphoreType.DMA((6,)),
            pltpu.SemaphoreType.DMA((6,)),
            pltpu.SemaphoreType.DMA((6,)),
            pltpu.SemaphoreType.DMA,
            pltpu.SemaphoreType.DMA,
            pltpu.SemaphoreType.DMA((FRAME,)),
            pltpu.SemaphoreType.DMA((FRAME,)),
            pltpu.SemaphoreType.DMA,
        ],
        compiler_params=pltpu.CompilerParams(
            collective_id=0, has_side_effects=True, vmem_limit_bytes=48 * 2**20
        ),
        name="grad_reduce_scatter",
    )(g, home)


def body(clip, gain, w_qkv, w_out, old_table, target_ids):
    frames_here, patches, width = clip.shape
    cols = w_qkv.shape[2]
    tokens = frames_here * patches
    each = tokens // FRAME

    ids = target_ids.reshape(tokens, 1)
    extra = jnp.concatenate([ids // 32, ids % 32, jnp.zeros((tokens, 126), jnp.int32)], axis=1)
    flat = jnp.concatenate([clip.reshape(tokens, width), extra.astype(bf16)], axis=1)
    t = iota((tokens, tokens), 0)
    pick = iota((tokens, tokens), 1) == (t % 2) * patches + (t // 8) * 4 + t % 8 // 2
    leaving = dot(pick.astype(bf16), flat).astype(bf16).reshape(FRAME, each, width + 128)
    arrived, w_other = gather_clip(leaving, w_out.reshape(2, cols // 2, width))

    home, g = sublayer(
        arrived.reshape(tokens, width + 128),
        gain.reshape(1, width),
        w_qkv,
        w_out,
        w_other.reshape(cols, width),
        old_table,
    )
    reduced, returned = reduce_scatter(g, home)

    t = iota((tokens, tokens), 0)
    source = (t % patches // 4) * 8 + (t % 4) * 2 + t // patches
    pick = iota((tokens, tokens), 1) == source
    d_clip = dot(pick.astype(bf16), returned.reshape(tokens, width)).astype(bf16)
    reduced = reduced[:ROWS].reshape(ROWS, 4, cols)
    return (
        d_clip.reshape(frames_here, patches, width),
        reduced[:, :3].transpose(1, 0, 2),
        reduced[:, 3].T,
    )


def solution(mesh):
    return jax.shard_map(
        body,
        mesh=mesh,
        in_specs=(
            P("frame", None, None),
            P(),
            P(None, None, "chan"),
            P("chan", None),
            P(),
            P("frame", None),
        ),
        out_specs=(P("frame", None, None), P(None, "frame", "chan"), P("chan", "frame")),
        check_vma=False,
    )
```

time: 419 us -> 193 us (0.46)
  Pallas kernels: 43.8 us -> 168 us
  blocking collectives: 104 us -> 0 us
  waiting for transfers between devices: 93.1 us -> 0 us
  matrix products: 55 us -> 5.65 us
  local copies, waits for them, and re-layouts: 66.2 us -> 18.6 us
  starting transfers between devices: 22.2 us -> 0 us
  other arithmetic: 19.1 us -> 0.08 us
  between operations: 14.4 us -> 0.81 us
    pallas_call x1 -> x3, Pallas kernels: 43.8 us -> 168 us  [the longest x1 68.3 us: sublayer(): pl.pallas_call(sublayer_kernel, out_shape=[jax.ShapeDtypeStruct((FRAME, 8...]
    all_gather x1 -> x0, blocking collectives: 104 us -> none  [body(): all_ids = lax.all_gather(target_ids, 'frame', axis=0, tiled=True)]
    psum x2 -> x0, waiting for transfers between devices: 93 us -> none  [the longest x1 47.2 us: body(): branch = lax.psum(part.astype(bf16), 'chan').astype(f32)]
    dot_general x11 -> x2, matrix products: 51.4 us -> 5.65 us  [dot(): return jnp.dot(a, b, preferred_element_type=f32)]
    reshape x7 -> x2, local copies, waits for them, and re-layouts: 29.6 us -> 0.83 us  [the longest x1 0.6 us: body(): gain.reshape(1, width)]
    all_to_all x2 -> x0, starting transfers between devices: 22 us -> none  [the longest x1 11.7 us: body(): lax.all_to_all(clip.reshape(frames_here, groups, patch_here, width), 'fra...]
    concatenate x1, local copies, waits for them, and re-layouts: 15.2 us -> 2.34 us  [body(): jnp.concatenate([clip.reshape(tokens, width), extra.astype(bf16)], axis=1)]
    concatenate x1 -> x0, other arithmetic: 7.65 us -> none  [body(): jnp.concatenate([g_qkv.astype(bf16), g_out.astype(bf16)[:, None]], axis=1)]
  transfers between devices with their start and end apart: 4 -> 0, of which waited for: 2 -> 0; matrix products, arithmetic and copies ran while one was open for 14% -> 0% of each run, Pallas kernels for 10% -> 0%
where the time goes in v2:
time: 193 us
  Pallas kernels  168 us (87%)
  local copies, waits for them, and re-layouts  18.6 us (10%)
  matrix products  5.65 us (3%)
    pallas_call x1, Pallas kernels, sublayer(): pl.pallas_call(sublayer_kernel, out_shape=[jax.ShapeDtypeStruct((FRAME, 8...  68.3 us
    pallas_call x1, Pallas kernels, reduce_scatter(): pl.pallas_call(reduce_scatter_kernel, out_shape=[jax.ShapeDtypeStruct(blo...  63.5 us
    pallas_call x1, Pallas kernels, gather_clip(): pl.pallas_call(gather_kernel, out_shape=[jax.ShapeDtypeStruct(src.shape,...  36.1 us
    unnamed x14, local copies, waits for them, and re-layouts  15 us
    dot_general x2, matrix products, dot(): return jnp.dot(a, b, preferred_element_type=f32)  5.65 us

profile of v2, /device:TPU:0, one launch (start us, length us, event | category | flops | bytes accessed | tf_op | source)
XLA Modules:
  0.0 193.0 jit_solution(7448454419005870188)
XLA Ops:
  0.6 0.7 copy.16
  1.4 0.2 copy.9
  1.5 0.2 copy.10
  1.8 2.3 %concatenate.6 = bf16[512,1536]{1,0:T(8,128)(2,1)S(1)} concatenate(bf16[512,1408]{1,0:T(8,128)(2,1)} %bitcast.29, bf16[512,1]{1,0:T(8,128)(2,1)S(1)} %copy.9, bf16[512,1]{1,0:T(8,128)(2,1)S(1)} %copy.10, bf16[512,126]{1,0:T(8,128)(2,1)S(1)} %broadcast_in_dim.3), dimensions={1} | concatenate | bytes 3145728 | tf_op jit(solution)/shard_map/concatenate | solution.py:515
  4.2 0.0 copy-start
  4.2 2.4 %fusion.src = bf16[64,8,1536]{2,1,0:T(8,128)(2,1)S(1)} fusion(bf16[512,1536]{1,0:T(8,128)(2,1)S(1)} %concatenate.6, s32[512]{0:T(512)S(1)} %get-tuple-element.18, s32[512]{0:T(512)S(1)} %get-tuple-element.21, s32[512]{0:T(512)S(1)} %get-tuple-element.17, s32[512]{0:T(512)S(1)} %get-tuple-element.22, s32[512]{0:T(512)S(1)} %get-tuple-element.19, ...), kind=kOutput, calls=%fused_computation.2 | convolution fusion | flops 812122112 | bytes 3159552 | tf_op jit(solution)/shard_map/dot_general | solution.py:138
  6.6 0.0 copy-done
  6.6 36.1 %gather_clip.1 = (bf16[64,8,1536]{2,1,0:T(8,128)(2,1)S(1)}, bf16[2,352,1408]{2,1,0:T(8,128)(2,1)S(1)}) custom-call(bf16[64,8,1536]{2,1,0:T(8,128)(2,1)S(1)} %fusion.src, bf16[2,352,1408]{2,1,0:T(8,128)(2,1)S(1)} %bitcast.25), custom_call_target="tpu_custom_call" | custom-call | tf_op jit(solution)/shard_map/gather_clip/pallas_call | solution.py:115
  42.7 0.0 copy-start.1
  42.7 1.3 copy-done.1
  44.0 0.0 copy-start.2
  44.0 1.2 copy-done.2
  45.2 9.1 %copy.11.w_qkv = bf16[3,1408,704]{2,1,0:T(8,128)(2,1)} copy(bf16[3,1408,704]{1,2,0:T(8,128)(2,1)} %param.8) | data formatting | bytes 11894784 | tf_op args[2]
  54.3 0.0 copy-done.4
  54.3 0.6 reshape.181.gain
  54.9 68.3 %sublayer.1 = (bf16[64,8,1408]{2,1,0:T(8,128)(2,1)}, bf16[2,4,2,4,24,2816]{5,4,3,2,1,0:T(8,128)(2,1)}) custom-call(bf16[512,1536]{1,0:T(8,128)(2,1)} %bitcast.27, bf16[1,1408]{1,0:T(2,128)(2,1)} %reshape.181.gain, bf16[3,1408,704]{2,1,0:T(8,128)(2,1)} %copy.11.w_qkv, bf16[704,1408]{1,0:T(8,128)(2,1)} %w_out.1, bf16[704,1408]{1,0:T(8,128)(2,1)} %bitcast.26, ...), custom_call_target="tpu_custom_call" | custom-call | tf_op jit(solution)/shard_map/sublayer/pallas_call | solution.py:312
  123.1 0.0 copy-start.3
  123.1 1.4 copy-done.3
  124.5 63.5 %grad_reduce_scatter.1 = (f32[24,2816]{1,0:T(8,128)S(1)}, bf16[64,8,1408]{2,1,0:T(8,128)(2,1)S(1)}) custom-call(bf16[2,4,2,4,24,2816]{5,4,3,2,1,0:T(8,128)(2,1)} %get-tuple-element.11.g, bf16[64,8,1408]{2,1,0:T(8,128)(2,1)S(1)} %copy-done.3), custom_call_target="tpu_custom_call" | custom-call | tf_op jit(solution)/shard_map/grad_reduce_scatter/pallas_call | solution.py:466
  188.0 3.3 %convolution_convert_fusion = bf16[512,1408]{1,0:T(8,128)(2,1)} fusion(bf16[64,8,1408]{2,1,0:T(8,128)(2,1)S(1)} %get-tuple-element.13, s32[512]{0:T(512)S(1)} %get-tuple-element.25, s32[512]{0:T(512)S(1)} %get-tuple-element.30, s32[512]{0:T(512)S(1)} %get-tuple-element.26, s32[512]{0:T(512)S(1)} %get-tuple-element.29, s32[512]{0:T(512)S(1)} %get-tuple-element.27, ...), kind=kOutput, calls=%fused_computation | convolution fusion | flops 744947712 | bytes 2897408 | tf_op jit(solution)/shard_map/dot_general | solution.py:138
  191.3 0.2 reshape.185
  191.5 0.7 copy.19
  192.3 0.1 slice.13
  192.3 0.6 copy.20
  (14 shorter events, 0.1 us)
Async XLA Ops:
  4.2 2.4 %copy-start = (bf16[704,1408]{1,0:T(8,128)(2,1)S(1)}, bf16[704,1408]{1,0:T(8,128)(2,1)}, u32[]{:S(2)}) copy-start(bf16[704,1408]{1,0:T(8,128)(2,1)} %w_out.1) | copy-start | bytes 5947396
  42.7 1.3 copy-start.1
  44.0 1.2 copy-start.2
  45.2 9.1 %copy-start.4 = (bf16[1408]{0:T(1024)(128)(2,1)S(1)}, bf16[1408]{0:T(1024)(128)(2,1)}, u32[]{:S(2)}) copy-start(bf16[1408]{0:T(1024)(128)(2,1)} %param.7) | copy-start | bytes 8452
  123.1 1.4 copy-start.3

commit v3 on v1

v3 whole, which is shorter than its diff:
```python
import jax
import jax.numpy as jnp
from jax import lax
from jax.experimental import pallas as pl
from jax.experimental.pallas import tpu as pltpu
from jax.sharding import PartitionSpec as P

HEAD_DIM = 88
EPS = 1e-05
VMEM_LIMIT = 63 * 2**20
XH, Y, Z, CORE = 2, 4, 4, 2
FRAME = XH * Y * Z * CORE
ROWS = 22
PAD = 24

f32 = jnp.float32
bf16 = jnp.bfloat16


def frame_index(xh, y, z, core):
    return ((xh * Y + y) * Z + z) * CORE + core


def coordinates():
    f = lax.axis_index("frame")
    return f // (Y * Z * CORE), (f // (Z * CORE)) % Y, (f // CORE) % Z, f % CORE


def all_peer(k):
    f = lax.axis_index("frame")
    chan = lax.axis_index("chan")
    p = (f + k) % FRAME
    far = (p // (FRAME // 2) + f // (FRAME // 2)) % 2
    return p, {"frame": p, "chan": (chan + far) % 2}


def greet_all(extras):
    barrier = pltpu.get_barrier_semaphore()

    def greet(k, _):
        pl.semaphore_signal(
            barrier, inc=1, device_id=all_peer(k)[1], device_id_type=pl.DeviceIdType.MESH
        )
        return 0

    lax.fori_loop(1, FRAME, greet, 0)
    for extra in extras:
        pl.semaphore_signal(barrier, inc=1, device_id=extra, device_id_type=pl.DeviceIdType.MESH)


def part(ref, i, width):
    return ref.at[i, :, pl.ds(0, width)]


def all_copy(src, dst, sends, recvs, k, width):
    p, peer = all_peer(k)
    return pltpu.make_async_remote_copy(
        src_ref=part(src, p, width), dst_ref=part(dst, lax.axis_index("frame"), width),
        send_sem=sends.at[k], recv_sem=recvs.at[k],
        device_id=peer, device_id_type=pl.DeviceIdType.MESH,
    )


def start_all(src, dst, sends, recvs, own_sem, width):
    def start(k, _):
        all_copy(src, dst, sends, recvs, k, width).start()
        return 0

    lax.fori_loop(1, FRAME, start, 0)
    f = lax.axis_index("frame")
    pltpu.make_async_copy(part(src, f, width), part(dst, f, width), own_sem).start()


def wait_all(src, dst, sends, recvs, own_sem, width):
    f = lax.axis_index("frame")
    pltpu.make_async_copy(part(src, f, width), part(dst, f, width), own_sem).wait()

    def wait(k, _):
        all_copy(src, dst, sends, recvs, k, width).wait_recv()
        return 0

    lax.fori_loop(1, FRAME, wait, 0)


def drain_all(src, dst, sends, recvs, width):
    def drain(k, _):
        all_copy(src, dst, sends, recvs, k, width).wait_send()
        return 0

    lax.fori_loop(1, FRAME, drain, 0)


def dot(a, b):
    return jnp.dot(a, b, preferred_element_type=f32)


def dot_nt(a, b):
    return lax.dot_general(a, b, (((1,), (1,)), ((), ())), preferred_element_type=f32)


def dot_tn(a, b):
    return lax.dot_general(a, b, (((0,), (0,)), ((), ())), preferred_element_type=f32)


def iota(shape, dim):
    return lax.broadcasted_iota(jnp.int32, shape, dim)


def norm_terms(x):
    centered = x - jnp.mean(x, axis=-1, keepdims=True)
    rstd = lax.rsqrt(jnp.mean(centered * centered, axis=-1, keepdims=True) + EPS)
    return centered * rstd, rstd


def add_blocks(out, terms, count):
    def step(j, _):
        total = terms[0][j].astype(f32)
        for t in terms[1:]:
            total = total + t[j].astype(f32)
        out[j] = total.astype(out.dtype)
        return 0

    lax.fori_loop(0, count, step, 0)


def layer_kernel(
    clip, ids, gain, w_qkv_hbm, w_out_hbm, table_hbm, out, d_recv,
    x_v, ids_v, leave, r, w_qkv, w_out, w_other, table,
    x_s, ids_s, n_s, qkv_s, o_s, oo_s, p_s, dy_s, do_s, d_s, dn_s, dno_s, n_t, dy_t,
    g, sib, r1, l1, r2, l2, r3, l3, br1, bl1, br2, bl2, br3, bl3, bmr, bml, u, xr,
    load_sem, w_sem, w_send, w_recv, own_sem, all_send, all_recv, home_own, home_send, home_recv,
    o_send, o_recv, dn_send, dn_recv,
    core_send, core_recv, a_send, a_recv, b_send, b_recv, x_send, x_recv,
):
    xh, y, z, core = coordinates()
    chan = lax.axis_index("chan")
    tokens, width = x_v.shape
    cols = o_s.shape[0]
    n_heads = cols // HEAD_DIM
    half = tokens // 2
    scale = HEAD_DIM ** (-0.5)
    here = y * (1 - core) + z * core
    there = z * (1 - core) + y * core

    def ring(first, step):
        dy = step if first else 0
        dz = 0 if first else step
        ny = (y + (1 - core) * dy + core * dz + Y) % Y
        nz = (z + core * dy + (1 - core) * dz + Z) % Z
        return {"frame": frame_index(xh, ny, nz, core)}

    sibling = {"frame": frame_index(xh, y, z, 1 - core)}
    across = {"frame": frame_index(1 - xh, y, z, core)}
    partner = {"chan": 1 - chan}

    def remote(src, dst, send, recv, peer):
        return pltpu.make_async_remote_copy(
            src_ref=src, dst_ref=dst, send_sem=send, recv_sem=recv,
            device_id=peer, device_id_type=pl.DeviceIdType.MESH,
        )

    loads = [
        pltpu.make_async_copy(clip, x_v, load_sem.at[0]),
        pltpu.make_async_copy(ids, ids_v, load_sem.at[1]),
        pltpu.make_async_copy(w_out_hbm, w_out, load_sem.at[2]),
        pltpu.make_async_copy(w_qkv_hbm, w_qkv, load_sem.at[3]),
        pltpu.make_async_copy(table_hbm, table, load_sem.at[4]),
    ]
    for c in loads:
        c.start()
    greet_all((partner, across))

    loads[0].wait()
    loads[1].wait()

    def leaving(j, _):
        t = iota((128, tokens), 0) + j * 128
        source = (t % 2) * half + (t // 8) * 4 + t % 8 // 2
        pick = (iota((128, tokens), 1) == source).astype(bf16)
        to = pl.ds(j * 16, 16)
        leave[to, :, :width] = dot(pick, x_v[...]).reshape(16, 8, width).astype(bf16)
        leave[to, :, width:] = dot(pick, ids_v[...]).reshape(16, 8, 128).astype(bf16)
        return 0

    lax.fori_loop(0, 4, leaving, 0)
    loads[2].wait()
    pl.semaphore_wait(pltpu.get_barrier_semaphore(), FRAME + 1)

    rows_half = cols // 2
    own_rows = pl.ds(pl.multiple_of(core * rows_half, 16), rows_half)
    w_first = remote(w_out.at[own_rows], w_other.at[own_rows], w_send.at[0], w_recv.at[0], partner)
    w_first.start()
    start_all(leave, r, all_send, all_recv, own_sem, width + 128)
    w_first.wait_recv()
    w_second = remote(
        w_other.at[own_rows], w_other.at[own_rows], w_send.at[1], w_recv.at[1], sibling
    )
    w_second.start()
    w_second.wait_recv()
    wait_all(leave, r, all_send, all_recv, own_sem, width + 128)
    loads[3].wait()
    loads[4].wait()

    def rows(c):
        return pl.ds(pl.multiple_of(c * half, half), half)

    def swap_o(c):
        return remote(o_s.at[:, rows(c)], oo_s.at[:, rows(c)], o_send.at[c], o_recv.at[c], partner)

    def swap_dn(c):
        return remote(dn_s.at[rows(c)], dno_s.at[rows(c)], dn_send.at[c], dn_recv.at[c], partner)

    def patch(c, pp):
        return pl.ds(pl.multiple_of(c * half + pp * 128, 128), 128)

    def forward(c, _):
        t = iota((half, tokens), 0)
        source = (t % 128 // 2) * 8 + 2 * (2 * c + t // 128) + t % 2
        pick = (iota((half, tokens), 1) == source).astype(bf16)
        moved = dot(pick, r[...].reshape(tokens, width + 128))
        x = moved[:, :width]
        x_s[rows(c), :] = x.astype(bf16)
        ids_s[rows(c), :] = moved[:, width:]
        xhat, _ = norm_terms(x)
        normed = (xhat * gain[...].astype(f32)).astype(bf16)
        n_s[rows(c), :] = normed
        for i in range(3):
            qkv = dot_nt(w_qkv[i * cols : (i + 1) * cols, :], normed)
            for h in range(n_heads):
                qkv_s[i * n_heads + h, :, rows(c)] = qkv[
                    h * HEAD_DIM : (h + 1) * HEAD_DIM
                ].astype(bf16)
        for pp in range(2):
            at = patch(c, pp)
            for h in range(n_heads):
                scores = dot_tn(qkv_s[n_heads + h, :, at], qkv_s[h, :, at]) * scale
                expo = jnp.exp(scores - jnp.max(scores, axis=0, keepdims=True))
                probs = expo * (1.0 / jnp.sum(expo, axis=0, keepdims=True))
                p_s[(2 * c + pp) * n_heads + h] = probs
                o_s[h * HEAD_DIM : (h + 1) * HEAD_DIM, at] = dot(
                    qkv_s[2 * n_heads + h, :, at], probs.astype(bf16)
                ).astype(bf16)
        swap_o(c).start()
        return 0

    lax.fori_loop(0, 2, forward, 0)

    block = 8 * ROWS
    window = 384

    def columns(source, target):
        for k in range(width // block):
            start = min(k * block // 128, (width - window) // 128) * 128
            shape = (8 * PAD, window)
            at = iota(shape, 0)
            wanted = jnp.where(
                at % PAD < ROWS, k * block + (at // PAD) * ROWS + at % PAD - start, -1
            )
            pick = (iota(shape, 1) == wanted).astype(bf16)
            picked = dot_nt(pick, source[:, start : start + window])
            for j in range(8):
                cj, zj = j % 2, j // 2
                a, b = (k % Y, zj) if cj == 0 else (zj, k % Y)
                to = (((cj * 4 + a) * 2 + k // Y) * 4 + b) * PAD
                target[to : to + PAD, :] = picked[j * PAD : (j + 1) * PAD].astype(bf16)

    def targets(c, _):
        hi_lo = ids_s[rows(c), :]
        wanted = hi_lo[:, 0:1] * 32.0 + hi_lo[:, 1:2]
        n_old = table.shape[0]
        pick = (iota((half, n_old), 1).astype(f32) == wanted).astype(bf16)
        x_v[rows(c), :] = dot(pick, table[...]).astype(bf16)
        return 0

    lax.fori_loop(0, 2, targets, 0)
    columns(n_s, n_t)

    def backward(c, _):
        swap_o(c).wait_recv()
        branch = dot_tn(o_s[:, rows(c)], w_out[...]) + dot_tn(oo_s[:, rows(c)], w_other[...])
        d_y = (x_s[rows(c), :].astype(f32) + branch - x_v[rows(c), :].astype(f32)).astype(bf16)
        dy_s[rows(c), :] = d_y
        d_o = dot_nt(w_out[...], d_y)
        for h in range(n_heads):
            do_s[h] = d_o[h * HEAD_DIM : (h + 1) * HEAD_DIM].astype(bf16)
        for pp in range(2):
            at = patch(c, pp)
            for h in range(n_heads):
                probs = p_s[(2 * c + pp) * n_heads + h]
                d_oh = do_s[h, :, pp * 128 : (pp + 1) * 128]
                dprobs = dot_tn(qkv_s[2 * n_heads + h, :, at], d_oh)
                rowsum = jnp.sum(dprobs * probs, axis=0, keepdims=True)
                ds = (probs * (dprobs - rowsum) * scale).astype(bf16)
                lo, hi = h * HEAD_DIM, (h + 1) * HEAD_DIM
                d_s[lo:hi, at] = dot(qkv_s[n_heads + h, :, at], ds).astype(bf16)
                d_s[cols + lo : cols + hi, at] = dot_nt(qkv_s[h, :, at], ds).astype(bf16)
                d_s[2 * cols + lo : 2 * cols + hi, at] = dot_nt(d_oh, probs.astype(bf16)).astype(
                    bf16
                )
        dn_s[rows(c), :] = dot_tn(d_s[:, rows(c)], w_qkv[...]).astype(bf16)
        swap_dn(c).start()
        return 0

    lax.fori_loop(0, 2, backward, 0)
    columns(dy_s, dy_t)

    def weight_grads(m):
        m = (m + 2 * (1 - core)) % 4
        at = pl.ds(pl.multiple_of(m * 16 * PAD, 16 * PAD), 16 * PAD)
        to = pl.ds(m * 16, 16)
        g[to, :, : 3 * cols] = (
            dot_nt(n_t[at, :], d_s[...]).reshape(16, PAD, 3 * cols).astype(bf16)
        )
        g[to, :, 3 * cols :] = dot_nt(dy_t[at, :], o_s[...]).reshape(16, PAD, cols).astype(bf16)

    def piece(c, a, h):
        return g.at[pl.ds(((c * 4 + a) * 2 + h) * 4, 4)]

    order = ((2, 0), (2, 1), (1, 1), (3, 0), (1, 0), (3, 1), (0, 0), (0, 1))
    mine = [piece(core, (here + da) % 4, h) for da, h in order]
    theirs = [piece(1 - core, (there + da) % 4, h) for da, h in order]
    lax.fori_loop(0, 2, lambda m, _: (weight_grads(m), 0)[1], 0)
    swaps = []
    for i in range(8):
        c = remote(theirs[i], sib.at[i], core_send.at[i], core_recv.at[i], sibling)
        c.start()
        swaps.append(c)
    lax.fori_loop(2, 4, lambda m, _: (weight_grads(m), 0)[1], 0)

    def fold(i):
        swaps[i].wait_recv()
        add_blocks(mine[i], (mine[i], sib.at[i]), 4)

    copies = []

    def send(src, dst, k, peer, sends, recvs):
        c = remote(src, dst, sends.at[k], recvs.at[k], peer)
        c.start()
        copies.append(c)
        return c

    right, left = ring(True, 1), ring(True, -1)
    fold(0)
    c1r = send(mine[0], r1, 0, right, a_send, a_recv)
    fold(1)
    c1l = send(mine[1], l1, 1, left, a_send, a_recv)
    fold(2)
    c2r = send(mine[2], r2, 2, right, a_send, a_recv)
    fold(3)
    c2l = send(mine[3], l2, 3, left, a_send, a_recv)
    fold(4)
    fold(5)
    fold(6)
    fold(7)

    drain_all(leave, r, all_send, all_recv, width + 128)

    def finish(c, _):
        swap_dn(c).wait_recv()
        dn = dn_s[rows(c), :].astype(f32) + dno_s[rows(c), :].astype(f32)
        xhat, rstd = norm_terms(x_s[rows(c), :].astype(f32))
        gs = dn * gain[...].astype(f32)
        back = rstd * (
            gs
            - jnp.mean(gs, axis=-1, keepdims=True)
            - xhat * jnp.mean(gs * xhat, axis=-1, keepdims=True)
        )
        x_v[rows(c), :] = (dy_s[rows(c), :].astype(f32) + back).astype(bf16)
        return 0

    lax.fori_loop(0, 2, finish, 0)

    def to_home(j, _):
        t = iota((128, tokens), 0) + j * 128
        source = (t % 8 // 2) * 128 + 2 * (t // 8) + t % 2
        pick = (iota((128, tokens), 1) == source).astype(bf16)
        leave[pl.ds(j * 16, 16), :, :width] = (
            dot(pick, x_v[...]).reshape(16, 8, width).astype(bf16)
        )
        return 0

    lax.fori_loop(0, 4, to_home, 0)
    start_all(leave, d_recv, home_send, home_recv, home_own, width)

    c1r.wait_recv()
    add_blocks(mine[4], (mine[4], r1), 4)
    c3r = send(mine[4], r3, 4, right, a_send, a_recv)
    c1l.wait_recv()
    add_blocks(mine[5], (mine[5], l1), 4)
    c3l = send(mine[5], l3, 5, left, a_send, a_recv)
    c2l.wait_recv()
    c3r.wait_recv()
    add_blocks(mine[6], (mine[6], r3, l2), 4)
    c2r.wait_recv()
    c3l.wait_recv()
    add_blocks(mine[7], (mine[7], r2, l3), 4)

    right, left = ring(False, 1), ring(False, -1)
    at = lambda h, d: g.at[((core * 4 + here) * 2 + h) * 4 + (there + d) % 4]
    d1r = send(at(0, 2), br1, 0, right, b_send, b_recv)
    d1l = send(at(1, 2), bl1, 1, left, b_send, b_recv)
    d2r = send(at(1, 1), br2, 2, right, b_send, b_recv)
    d2l = send(at(0, 3), bl2, 3, left, b_send, b_recv)
    d1r.wait_recv()
    bmr[...] = (at(0, 1)[...].astype(f32) + br1[...].astype(f32)).astype(bf16)
    d3r = send(bmr, br3, 4, right, b_send, b_recv)
    d1l.wait_recv()
    bml[...] = (at(1, 3)[...].astype(f32) + bl1[...].astype(f32)).astype(bf16)
    d3l = send(bml, bl3, 5, left, b_send, b_recv)
    d2l.wait_recv()
    d3r.wait_recv()
    u[0] = (at(0, 0)[...].astype(f32) + br3[...].astype(f32) + bl2[...].astype(f32)).astype(bf16)
    d2r.wait_recv()
    d3l.wait_recv()
    u[1] = (at(1, 0)[...].astype(f32) + br2[...].astype(f32) + bl3[...].astype(f32)).astype(bf16)

    e = remote(u.at[1 - xh], xr, x_send, x_recv, across)
    e.start()
    e.wait_recv()
    out[...] = u[xh].astype(f32) + xr[...].astype(f32)
    wait_all(leave, d_recv, home_send, home_recv, home_own, width)

    e.wait_send()
    w_first.wait_send()
    w_second.wait_send()
    for c in swaps:
        c.wait_send()
    for c in copies:
        c.wait_send()
    for c in range(2):
        swap_o(c).wait_send()
        swap_dn(c).wait_send()
    drain_all(leave, d_recv, home_send, home_recv, width)


def layer(clip, ids, gain, w_qkv, w_out, table):
    tokens, width = clip.shape
    cols = w_out.shape[0]
    n_heads = cols // HEAD_DIM
    each = tokens // FRAME
    vmem = pl.BlockSpec(memory_space=pltpu.VMEM)
    anywhere = pl.BlockSpec(memory_space=pl.ANY)
    wide = pltpu.VMEM((tokens, width), bf16)
    narrow = pltpu.VMEM((cols, tokens), bf16)
    piece = pltpu.VMEM((4, PAD, 4 * cols), bf16)
    block = pltpu.VMEM((PAD, 4 * cols), bf16)
    carry = pltpu.VMEM((FRAME, each, width + 128), bf16)
    dma = pltpu.SemaphoreType.DMA
    return pl.pallas_call(
        layer_kernel,
        out_shape=[
            jax.ShapeDtypeStruct((PAD, 4 * cols), f32),
            jax.ShapeDtypeStruct((FRAME, each, width), bf16),
        ],
        in_specs=[anywhere, anywhere, vmem, anywhere, anywhere, anywhere],
        out_specs=[vmem, vmem],
        scratch_shapes=[
            wide,
            pltpu.VMEM((tokens, 128), bf16),
            carry,
            carry,
            pltpu.VMEM((3 * cols, width), bf16),
            pltpu.VMEM((cols, width), bf16),
            pltpu.VMEM((cols, width), bf16),
            pltpu.VMEM(table.shape, bf16),
            wide,
            pltpu.VMEM((tokens, 128), f32),
            wide,
            pltpu.VMEM((3 * n_heads, HEAD_DIM, tokens), bf16),
            narrow,
            narrow,
            pltpu.VMEM((tokens // 128 * n_heads, 128, 128), f32),
            wide,
            pltpu.VMEM((n_heads, HEAD_DIM, tokens // 2), bf16),
            pltpu.VMEM((3 * cols, tokens), bf16),
            wide,
            wide,
            pltpu.VMEM((FRAME * PAD, tokens), bf16),
            pltpu.VMEM((FRAME * PAD, tokens), bf16),
            pltpu.VMEM((FRAME, PAD, 4 * cols), bf16),
            pltpu.VMEM((8, 4, PAD, 4 * cols), bf16),
        ]
        + [piece] * 6
        + [block] * 8
        + [pltpu.VMEM((2, PAD, 4 * cols), bf16), block]
        + [
            dma((5,)), dma, dma((2,)), dma((2,)),
            dma, dma((FRAME,)), dma((FRAME,)), dma, dma((FRAME,)), dma((FRAME,)),
            dma((2,)), dma((2,)), dma((2,)), dma((2,)),
            dma((8,)), dma((8,)), dma((6,)), dma((6,)), dma((6,)), dma((6,)), dma, dma,
        ],
        compiler_params=pltpu.CompilerParams(
            collective_id=0, has_side_effects=True, vmem_limit_bytes=VMEM_LIMIT
        ),
        name="layer",
    )(clip, ids, gain, w_qkv, w_out, table)


def body(clip, gain, w_qkv, w_out, old_table, target_ids):
    frames_here, patches, width = clip.shape
    cols = w_qkv.shape[2]
    tokens = frames_here * patches

    ids = target_ids.reshape(tokens, 1)
    lane = iota((tokens, 128), 1)
    ids = jnp.where(lane == 0, ids // 32, jnp.where(lane == 1, ids % 32, 0)).astype(bf16)
    reduced, returned = layer(
        clip.reshape(tokens, width),
        ids,
        gain.reshape(1, width),
        w_qkv.transpose(0, 2, 1).reshape(3 * cols, width),
        w_out,
        old_table,
    )

    t = iota((tokens, tokens), 0)
    source = (t % patches // 4) * 8 + (t % 4) * 2 + t // patches
    pick = iota((tokens, tokens), 1) == source
    d_clip = dot(pick.astype(bf16), returned.reshape(tokens, width)).astype(bf16)
    reduced = reduced[:ROWS].reshape(ROWS, 4, cols)
    return (
        d_clip.reshape(frames_here, patches, width),
        reduced[:, :3].transpose(1, 0, 2),
        reduced[:, 3].T,
    )


def solution(mesh):
    return jax.shard_map(
        body,
        mesh=mesh,
        in_specs=(
            P("frame", None, None),
            P(),
            P(None, None, "chan"),
            P("chan", None),
            P(),
            P("frame", None),
        ),
        out_specs=(P("frame", None, None), P(None, "frame", "chan"), P("chan", "frame")),
        check_vma=False,
    )
```

time: 419 us -> 157 us (0.37)
  the two profiles are of different devices: /device:TPU:0 before, /device:TPU:52 now
where the time goes in v3:
time: 157 us
  Pallas kernels  147 us (94%)
  matrix products  4.65 us (3%)
  local copies, waits for them, and re-layouts  3.65 us (2%)
    pallas_call x1, Pallas kernels, layer(): pl.pallas_call(layer_kernel, out_shape=[jax.ShapeDtypeStruct((PAD, 4 * co...  147 us
    dot_general x1, matrix products, dot(): return jnp.dot(a, b, preferred_element_type=f32)  4.65 us

profile of v3, /device:TPU:52, one launch (start us, length us, event | category | flops | bytes accessed | tf_op | source)
XLA Modules:
  0.0 156.9 jit_solution(6350713481878816207)
XLA Ops:
  0.7 0.7 copy.13
  1.4 1.3 reshape.116.gain
  2.7 0.9 select_convert_fusion.ids
  3.5 147.0 %layer.1 = (f32[24,2816]{1,0:T(8,128)}, bf16[64,8,1408]{2,1,0:T(8,128)(2,1)}) custom-call(bf16[512,1408]{1,0:T(8,128)(2,1)} %bitcast.21, bf16[512,128]{1,0:T(8,128)(2,1)} %select_convert_fusion.ids, bf16[1,1408]{1,0:T(2,128)(2,1)} %reshape.116.gain, bf16[2112,1408]{1,0:T(8,128)(2,1)} %bitcast.20, bf16[704,1408]{1,0:T(8,128)(2,1)} %w_out_hbm.1, ...), custom_call_target="tpu_custom_call" | custom-call | tf_op jit(solution)/shard_map/layer/pallas_call | solution.py:449
  150.5 0.0 copy-start
  150.5 4.7 %convolution_convert_fusion = bf16[512,1408]{1,0:T(8,128)(2,1)} fusion(bf16[64,8,1408]{2,1,0:T(8,128)(2,1)} %get-tuple-element.5, s32[512]{0:T(512)S(1)} %get-tuple-element.11, s32[512]{0:T(512)S(1)} %get-tuple-element.16, s32[512]{0:T(512)S(1)} %get-tuple-element.12, s32[512]{0:T(512)S(1)} %get-tuple-element.15, s32[512]{0:T(512)S(1)} %get-tuple-element.13, ...), kind=kOutput, calls=%fused_computation | convolution fusion | flops 744947712 | bytes 2897408 | tf_op jit(solution)/shard_map/dot_general | solution.py:94
  155.2 0.0 copy-done
  155.2 0.2 reshape.120
  155.4 0.1 slice.13
  155.5 0.6 copy.17
  156.2 0.7 copy.16
  (7 shorter events, 0.0 us)
Async XLA Ops:
  150.5 4.7 %copy-start = (f32[24,2816]{1,0:T(8,128)S(1)}, f32[24,2816]{1,0:T(8,128)}, u32[]{:S(2)}) copy-start(f32[24,2816]{1,0:T(8,128)} %get-tuple-element.6) | copy-start | bytes 811012

commit v4 on v3

--- a/solution.py
+++ b/solution.py
@@ -1,3 +1,5 @@
+import functools
+
 import jax
 import jax.numpy as jnp
 from jax import lax
@@ -10,6 +12,7 @@
 VMEM_LIMIT = 63 * 2**20
 XH, Y, Z, CORE = 2, 4, 4, 2
 FRAME = XH * Y * Z * CORE
+CHAN = 2
 ROWS = 22
 PAD = 24
 
@@ -34,18 +37,19 @@
     return p, {"frame": p, "chan": (chan + far) % 2}
 
 
-def greet_all(extras):
+def greet_all():
     barrier = pltpu.get_barrier_semaphore()
+    me = lax.axis_index("frame") * CHAN + lax.axis_index("chan")
 
     def greet(k, _):
+        other = (me + k) % (FRAME * CHAN)
         pl.semaphore_signal(
-            barrier, inc=1, device_id=all_peer(k)[1], device_id_type=pl.DeviceIdType.MESH
+            barrier, inc=1, device_id={"frame": other // CHAN, "chan": other % CHAN},
+            device_id_type=pl.DeviceIdType.MESH,
         )
         return 0
 
-    lax.fori_loop(1, FRAME, greet, 0)
-    for extra in extras:
-        pl.semaphore_signal(barrier, inc=1, device_id=extra, device_id_type=pl.DeviceIdType.MESH)
+    lax.fori_loop(1, FRAME * CHAN, greet, 0)
 
 
 def part(ref, i, width):
@@ -102,6 +106,14 @@
     return lax.dot_general(a, b, (((0,), (0,)), ((), ())), preferred_element_type=f32)
 
 
+def alone(run):
+    def once(i, _):
+        run()
+        return 0
+
+    lax.fori_loop(0, lax.axis_index("chan") // 2 + 1, once, 0)
+
+
 def iota(shape, dim):
     return lax.broadcasted_iota(jnp.int32, shape, dim)
 
@@ -126,7 +138,7 @@
 def layer_kernel(
     clip, ids, gain, w_qkv_hbm, w_out_hbm, table_hbm, out, d_recv,
     x_v, ids_v, leave, r, w_qkv, w_out, w_other, table,
-    x_s, ids_s, n_s, qkv_s, o_s, oo_s, p_s, dy_s, do_s, d_s, dn_s, dno_s, n_t, dy_t,
+    x_s, ids_s, n_s, qkv_s, o_s, oo_s, p_s, dy_s, do_s, ds_s, d_s, dn_s, dno_s, n_t, dy_t,
     g, sib, r1, l1, r2, l2, r3, l3, br1, bl1, br2, bl2, br3, bl3, bmr, bml, u, xr,
     load_sem, w_sem, w_send, w_recv, own_sem, all_send, all_recv, home_own, home_send, home_recv,
     o_send, o_recv, dn_send, dn_recv,
@@ -139,6 +151,7 @@
     n_heads = cols // HEAD_DIM
     half = tokens // 2
     scale = HEAD_DIM ** (-0.5)
+    kept = (xh + chan + core) % 2
     here = y * (1 - core) + z * core
     there = z * (1 - core) + y * core
 
@@ -168,7 +181,7 @@
     ]
     for c in loads:
         c.start()
-    greet_all((partner, across))
+    greet_all()
 
     loads[0].wait()
     loads[1].wait()
@@ -184,19 +197,13 @@
 
     lax.fori_loop(0, 4, leaving, 0)
     loads[2].wait()
-    pl.semaphore_wait(pltpu.get_barrier_semaphore(), FRAME + 1)
+    pl.semaphore_wait(pltpu.get_barrier_semaphore(), FRAME * CHAN - 1)
 
     rows_half = cols // 2
     own_rows = pl.ds(pl.multiple_of(core * rows_half, 16), rows_half)
     w_first = remote(w_out.at[own_rows], w_other.at[own_rows], w_send.at[0], w_recv.at[0], partner)
     w_first.start()
     start_all(leave, r, all_send, all_recv, own_sem, width + 128)
-    w_first.wait_recv()
-    w_second = remote(
-        w_other.at[own_rows], w_other.at[own_rows], w_send.at[1], w_recv.at[1], sibling
-    )
-    w_second.start()
-    w_second.wait_recv()
     wait_all(leave, r, all_send, all_recv, own_sem, width + 128)
     loads[3].wait()
     loads[4].wait()
@@ -208,7 +215,10 @@
         return remote(o_s.at[:, rows(c)], oo_s.at[:, rows(c)], o_send.at[c], o_recv.at[c], partner)
 
     def swap_dn(c):
-        return remote(dn_s.at[rows(c)], dno_s.at[rows(c)], dn_send.at[c], dn_recv.at[c], partner)
+        two = pl.ds(2 * c, 2)
+        return remote(
+            dn_s.at[two, 1 - kept], dno_s.at[two], dn_send.at[c], dn_recv.at[c], partner
+        )
 
     def patch(c, pp):
         return pl.ds(pl.multiple_of(c * half + pp * 128, 128), 128)
@@ -230,6 +240,11 @@
                 qkv_s[i * n_heads + h, :, rows(c)] = qkv[
                     h * HEAD_DIM : (h + 1) * HEAD_DIM
                 ].astype(bf16)
+        alone(functools.partial(forward_heads, c))
+        swap_o(c).start()
+        return 0
+
+    def forward_heads(c):
         for pp in range(2):
             at = patch(c, pp)
             for h in range(n_heads):
@@ -240,8 +255,6 @@
                 o_s[h * HEAD_DIM : (h + 1) * HEAD_DIM, at] = dot(
                     qkv_s[2 * n_heads + h, :, at], probs.astype(bf16)
                 ).astype(bf16)
-        swap_o(c).start()
-        return 0
 
     lax.fori_loop(0, 2, forward, 0)
 
@@ -272,8 +285,14 @@
         x_v[rows(c), :] = dot(pick, table[...]).astype(bf16)
         return 0
 
+    w_first.wait_recv()
+    w_second = remote(
+        w_other.at[own_rows], w_other.at[own_rows], w_send.at[1], w_recv.at[1], sibling
+    )
+    w_second.start()
     lax.fori_loop(0, 2, targets, 0)
     columns(n_s, n_t)
+    w_second.wait_recv()
 
     def backward(c, _):
         swap_o(c).wait_recv()
@@ -283,6 +302,14 @@
         d_o = dot_nt(w_out[...], d_y)
         for h in range(n_heads):
             do_s[h] = d_o[h * HEAD_DIM : (h + 1) * HEAD_DIM].astype(bf16)
+        alone(functools.partial(score_heads, c))
+        alone(functools.partial(value_heads, c))
+        dn = dot_tn(d_s[:, rows(c)], w_qkv[...])
+        dn_s[pl.ds(2 * c, 2)] = dn.reshape(2, 2, 64, width).astype(bf16)
+        swap_dn(c).start()
+        return 0
+
+    def score_heads(c):
         for pp in range(2):
             at = patch(c, pp)
             for h in range(n_heads):
@@ -291,15 +318,22 @@
                 dprobs = dot_tn(qkv_s[2 * n_heads + h, :, at], d_oh)
                 rowsum = jnp.sum(dprobs * probs, axis=0, keepdims=True)
                 ds = (probs * (dprobs - rowsum) * scale).astype(bf16)
+                ds_s[pp * n_heads + h] = ds
+                d_s[h * HEAD_DIM : (h + 1) * HEAD_DIM, at] = dot(
+                    qkv_s[n_heads + h, :, at], ds
+                ).astype(bf16)
+
+    def value_heads(c):
+        for pp in range(2):
+            at = patch(c, pp)
+            for h in range(n_heads):
                 lo, hi = h * HEAD_DIM, (h + 1) * HEAD_DIM
-                d_s[lo:hi, at] = dot(qkv_s[n_heads + h, :, at], ds).astype(bf16)
-                d_s[cols + lo : cols + hi, at] = dot_nt(qkv_s[h, :, at], ds).astype(bf16)
-                d_s[2 * cols + lo : 2 * cols + hi, at] = dot_nt(d_oh, probs.astype(bf16)).astype(
-                    bf16
-                )
-        dn_s[rows(c), :] = dot_tn(d_s[:, rows(c)], w_qkv[...]).astype(bf16)
-        swap_dn(c).start()
-        return 0
+                probs = p_s[(2 * c + pp) * n_heads + h].astype(bf16)
+                d_oh = do_s[h, :, pp * 128 : (pp + 1) * 128]
+                d_s[cols + lo : cols + hi, at] = dot_nt(
+                    qkv_s[h, :, at], ds_s[pp * n_heads + h]
+                ).astype(bf16)
+                d_s[2 * cols + lo : 2 * cols + hi, at] = dot_nt(d_oh, probs).astype(bf16)
 
     lax.fori_loop(0, 2, backward, 0)
     columns(dy_s, dy_t)
@@ -355,32 +389,71 @@
 
     drain_all(leave, r, all_send, all_recv, width + 128)
 
-    def finish(c, _):
-        swap_dn(c).wait_recv()
-        dn = dn_s[rows(c), :].astype(f32) + dno_s[rows(c), :].astype(f32)
-        xhat, rstd = norm_terms(x_s[rows(c), :].astype(f32))
+    def finish(p, _):
+        @pl.when(p % 2 == 0)
+        def _():
+            swap_dn(p // 2).wait_recv()
+
+        at = pl.ds(pl.multiple_of(p * 128 + kept * 64, 64), 64)
+        dn = dn_s[p, kept].astype(f32) + dno_s[p].astype(f32)
+        xhat, rstd = norm_terms(x_s[at, :].astype(f32))
         gs = dn * gain[...].astype(f32)
         back = rstd * (
             gs
             - jnp.mean(gs, axis=-1, keepdims=True)
             - xhat * jnp.mean(gs * xhat, axis=-1, keepdims=True)
         )
-        x_v[rows(c), :] = (dy_s[rows(c), :].astype(f32) + back).astype(bf16)
-        return 0
-
-    lax.fori_loop(0, 2, finish, 0)
+        x_v[pl.ds(pl.multiple_of(p * 64, 64), 64), :] = (
+            dy_s[at, :].astype(f32) + back
+        ).astype(bf16)
+        return 0
+
+    lax.fori_loop(0, 4, finish, 0)
 
     def to_home(j, _):
-        t = iota((128, tokens), 0) + j * 128
-        source = (t % 8 // 2) * 128 + 2 * (t // 8) + t % 2
-        pick = (iota((128, tokens), 1) == source).astype(bf16)
+        t = iota((128, half), 0) + j * 128
+        source = (t % 8 // 2) * 64 + 2 * (t // 8) + t % 2
+        pick = (iota((128, half), 1) == source).astype(bf16)
         leave[pl.ds(j * 16, 16), :, :width] = (
-            dot(pick, x_v[...]).reshape(16, 8, width).astype(bf16)
+            dot(pick, x_v[pl.ds(0, half), :]).reshape(16, 8, width).astype(bf16)
         )
         return 0
 
-    lax.fori_loop(0, 4, to_home, 0)
-    start_all(leave, d_recv, home_send, home_recv, home_own, width)
+    lax.fori_loop(0, 2, to_home, 0)
+
+    f = lax.axis_index("frame")
+    own = (kept + xh) % 2 == 0
+
+    def home_copy(k, c):
+        q = (f + k) % (FRAME // 2)
+        return pltpu.make_async_remote_copy(
+            src_ref=part(leave, q, width), dst_ref=d_recv.at[f],
+            send_sem=home_send.at[2 * k + c], recv_sem=home_recv.at[2 * k + c],
+            device_id={"frame": kept * (FRAME // 2) + q, "chan": (chan + c) % 2},
+            device_id_type=pl.DeviceIdType.MESH,
+        )
+
+    home_local = pltpu.make_async_copy(part(leave, f % (FRAME // 2), width), d_recv.at[f], home_own)
+
+    def home_each(run, run_own):
+        @pl.when(own)
+        def _():
+            run_own()
+
+        @pl.when(jnp.logical_not(own))
+        def _():
+            run(home_copy(0, 0))
+
+        run(home_copy(0, 1))
+
+        def step(k, _):
+            run(home_copy(k, 0))
+            run(home_copy(k, 1))
+            return 0
+
+        lax.fori_loop(1, FRAME // 2, step, 0)
+
+    home_each(lambda c: c.start(), home_local.start)
 
     c1r.wait_recv()
     add_blocks(mine[4], (mine[4], r1), 4)
@@ -418,7 +491,7 @@
     e.start()
     e.wait_recv()
     out[...] = u[xh].astype(f32) + xr[...].astype(f32)
-    wait_all(leave, d_recv, home_send, home_recv, home_own, width)
+    home_each(lambda c: c.wait_recv(), home_local.wait)
 
     e.wait_send()
     w_first.wait_send()
@@ -430,7 +503,7 @@
     for c in range(2):
         swap_o(c).wait_send()
         swap_dn(c).wait_send()
-    drain_all(leave, d_recv, home_send, home_recv, width)
+    home_each(lambda c: c.wait_send(), lambda: None)
 
 
 def layer(clip, ids, gain, w_qkv, w_out, table):
@@ -472,9 +545,10 @@
             pltpu.VMEM((tokens // 128 * n_heads, 128, 128), f32),
             wide,
             pltpu.VMEM((n_heads, HEAD_DIM, tokens // 2), bf16),
+            pltpu.VMEM((2 * n_heads, 128, 128), bf16),
             pltpu.VMEM((3 * cols, tokens), bf16),
-            wide,
-            wide,
+            pltpu.VMEM((4, 2, 64, width), bf16),
+            pltpu.VMEM((4, 64, width), bf16),
             pltpu.VMEM((FRAME * PAD, tokens), bf16),
             pltpu.VMEM((FRAME * PAD, tokens), bf16),
             pltpu.VMEM((FRAME, PAD, 4 * cols), bf16),

time: 157 us -> 139 us (0.89)
  the two profiles are of different devices: /device:TPU:52 before, /device:TPU:0 now
where the time goes in v4:
time: 139 us; the launch traced here: 138 us
  Pallas kernels  128 us (92%)
  matrix products  4.65 us (3%)
  local copies, waits for them, and re-layouts  3.65 us (3%)
    pallas_call x1, Pallas kernels, layer(): pl.pallas_call(layer_kernel, out_shape=[jax.ShapeDtypeStruct((PAD, 4 * co...  128 us
    dot_general x1, matrix products, dot(): return jnp.dot(a, b, preferred_element_type=f32)  4.65 us

profile of v4, /device:TPU:0, one launch (start us, length us, event | category | flops | bytes accessed | tf_op | source)
XLA Modules:
  0.0 137.9 jit_solution(15984708289238536968)
XLA Ops:
  0.7 0.7 copy.13
  1.4 1.3 reshape.116.gain
  2.7 0.9 select_convert_fusion.ids
  3.5 128.0 %layer.1 = (f32[24,2816]{1,0:T(8,128)}, bf16[64,8,1408]{2,1,0:T(8,128)(2,1)}) custom-call(bf16[512,1408]{1,0:T(8,128)(2,1)} %bitcast.21, bf16[512,128]{1,0:T(8,128)(2,1)} %select_convert_fusion.ids, bf16[1,1408]{1,0:T(2,128)(2,1)} %reshape.116.gain, bf16[2112,1408]{1,0:T(8,128)(2,1)} %bitcast.20, bf16[704,1408]{1,0:T(8,128)(2,1)} %w_out_hbm.1, ...), custom_call_target="tpu_custom_call" | custom-call | tf_op jit(solution)/shard_map/layer/pallas_call | solution.py:522
  131.5 0.0 copy-start
  131.5 4.7 %convolution_convert_fusion = bf16[512,1408]{1,0:T(8,128)(2,1)} fusion(bf16[64,8,1408]{2,1,0:T(8,128)(2,1)} %get-tuple-element.5, s32[512]{0:T(512)S(1)} %get-tuple-element.11, s32[512]{0:T(512)S(1)} %get-tuple-element.16, s32[512]{0:T(512)S(1)} %get-tuple-element.12, s32[512]{0:T(512)S(1)} %get-tuple-element.15, s32[512]{0:T(512)S(1)} %get-tuple-element.13, ...), kind=kOutput, calls=%fused_computation | convolution fusion | flops 744947712 | bytes 2897408 | tf_op jit(solution)/shard_map/dot_general | solution.py:98
  136.2 0.0 copy-done
  136.2 0.2 reshape.120
  136.4 0.1 slice.13
  136.5 0.6 copy.17
  137.1 0.7 copy.16
  (7 shorter events, 0.0 us)
Async XLA Ops:
  131.5 4.7 %copy-start = (f32[24,2816]{1,0:T(8,128)S(1)}, f32[24,2816]{1,0:T(8,128)}, u32[]{:S(2)}) copy-start(f32[24,2816]{1,0:T(8,128)} %get-tuple-element.6) | copy-start | bytes 811012

commit v5 on v4

--- a/solution.py
+++ b/solution.py
@@ -37,19 +37,15 @@
     return p, {"frame": p, "chan": (chan + far) % 2}
 
 
-def greet_all():
-    barrier = pltpu.get_barrier_semaphore()
+def greet(k):
     me = lax.axis_index("frame") * CHAN + lax.axis_index("chan")
-
-    def greet(k, _):
-        other = (me + k) % (FRAME * CHAN)
-        pl.semaphore_signal(
-            barrier, inc=1, device_id={"frame": other // CHAN, "chan": other % CHAN},
-            device_id_type=pl.DeviceIdType.MESH,
-        )
-        return 0
-
-    lax.fori_loop(1, FRAME * CHAN, greet, 0)
+    other = (me + k) % (FRAME * CHAN)
+    pl.semaphore_signal(
+        pltpu.get_barrier_semaphore(),
+        inc=1,
+        device_id={"frame": other // CHAN, "chan": other % CHAN},
+        device_id_type=pl.DeviceIdType.MESH,
+    )
 
 
 def part(ref, i, width):
@@ -136,13 +132,13 @@
 
 
 def layer_kernel(
-    clip, ids, gain, w_qkv_hbm, w_out_hbm, table_hbm, out, d_recv,
-    x_v, ids_v, leave, r, w_qkv, w_out, w_other, table,
+    clip, ids, gain, w_qkv_hbm, w_out_hbm, table_hbm, out, d_clip,
+    d_recv, x_v, ids_v, leave, r, w_qkv, w_out, w_other, table,
     x_s, ids_s, n_s, qkv_s, o_s, oo_s, p_s, dy_s, do_s, ds_s, d_s, dn_s, dno_s, n_t, dy_t,
-    g, sib, r1, l1, r2, l2, r3, l3, br1, bl1, br2, bl2, br3, bl3, bmr, bml, u, xr,
+    nt_x, dyt_x, d_x, o_x, g, r1, l1, r2, l2, r3, l3, br1, bl1, br2, bl2, br3, bl3, bmr, bml, u, xr,
     load_sem, w_sem, w_send, w_recv, own_sem, all_send, all_recv, home_own, home_send, home_recv,
     o_send, o_recv, dn_send, dn_recv,
-    core_send, core_recv, a_send, a_recv, b_send, b_recv, x_send, x_recv,
+    ox_sems, ntx_sems, dyx_sems, dx_sems, a_send, a_recv, b_send, b_recv, x_send, x_recv,
 ):
     xh, y, z, core = coordinates()
     chan = lax.axis_index("chan")
@@ -181,7 +177,11 @@
     ]
     for c in loads:
         c.start()
-    greet_all()
+    def greet_some(k, _):
+        greet(k)
+        return 0
+
+    lax.fori_loop(1, FRAME * CHAN, greet_some, 0)
 
     loads[0].wait()
     loads[1].wait()
@@ -219,6 +219,25 @@
         return remote(
             dn_s.at[two, 1 - kept], dno_s.at[two], dn_send.at[c], dn_recv.at[c], partner
         )
+
+    half_rows = FRAME * PAD // 2
+    theirs = pl.ds(pl.multiple_of((1 - core) * half_rows, half_rows), half_rows)
+    ours = pl.ds(pl.multiple_of(core * half_rows, half_rows), half_rows)
+
+    def swap_core(src, dst, sems, c):
+        return remote(src, dst, sems.at[0, c], sems.at[1, c], sibling)
+
+    def swap_ox(c):
+        return swap_core(o_s.at[:, rows(c)], o_x.at[:, rows(c)], ox_sems, c)
+
+    def swap_ntx(c):
+        return swap_core(n_t.at[theirs, rows(c)], nt_x.at[:, rows(c)], ntx_sems, c)
+
+    def swap_dyx(c):
+        return swap_core(dy_t.at[theirs, rows(c)], dyt_x.at[:, rows(c)], dyx_sems, c)
+
+    def swap_dx(c):
+        return swap_core(d_s.at[:, rows(c)], d_x.at[:, rows(c)], dx_sems, c)
 
     def patch(c, pp):
         return pl.ds(pl.multiple_of(c * half + pp * 128, 128), 128)
@@ -242,6 +261,7 @@
                 ].astype(bf16)
         alone(functools.partial(forward_heads, c))
         swap_o(c).start()
+        swap_ox(c).start()
         return 0
 
     def forward_heads(c):
@@ -261,7 +281,7 @@
     block = 8 * ROWS
     window = 384
 
-    def columns(source, target):
+    def columns(source, target, c):
         for k in range(width // block):
             start = min(k * block // 128, (width - window) // 128) * 128
             shape = (8 * PAD, window)
@@ -270,12 +290,12 @@
                 at % PAD < ROWS, k * block + (at // PAD) * ROWS + at % PAD - start, -1
             )
             pick = (iota(shape, 1) == wanted).astype(bf16)
-            picked = dot_nt(pick, source[:, start : start + window])
+            picked = dot_nt(pick, source[rows(c), start : start + window])
             for j in range(8):
                 cj, zj = j % 2, j // 2
                 a, b = (k % Y, zj) if cj == 0 else (zj, k % Y)
                 to = (((cj * 4 + a) * 2 + k // Y) * 4 + b) * PAD
-                target[to : to + PAD, :] = picked[j * PAD : (j + 1) * PAD].astype(bf16)
+                target[to : to + PAD, rows(c)] = picked[j * PAD : (j + 1) * PAD].astype(bf16)
 
     def targets(c, _):
         hi_lo = ids_s[rows(c), :]
@@ -283,6 +303,8 @@
         n_old = table.shape[0]
         pick = (iota((half, n_old), 1).astype(f32) == wanted).astype(bf16)
         x_v[rows(c), :] = dot(pick, table[...]).astype(bf16)
+        alone(functools.partial(columns, n_s, n_t, c))
+        swap_ntx(c).start()
         return 0
 
     w_first.wait_recv()
@@ -291,7 +313,6 @@
     )
     w_second.start()
     lax.fori_loop(0, 2, targets, 0)
-    columns(n_s, n_t)
     w_second.wait_recv()
 
     def backward(c, _):
@@ -299,11 +320,14 @@
         branch = dot_tn(o_s[:, rows(c)], w_out[...]) + dot_tn(oo_s[:, rows(c)], w_other[...])
         d_y = (x_s[rows(c), :].astype(f32) + branch - x_v[rows(c), :].astype(f32)).astype(bf16)
         dy_s[rows(c), :] = d_y
+        alone(functools.partial(columns, dy_s, dy_t, c))
+        swap_dyx(c).start()
         d_o = dot_nt(w_out[...], d_y)
         for h in range(n_heads):
             do_s[h] = d_o[h * HEAD_DIM : (h + 1) * HEAD_DIM].astype(bf16)
         alone(functools.partial(score_heads, c))
         alone(functools.partial(value_heads, c))
+        swap_dx(c).start()
         dn = dot_tn(d_s[:, rows(c)], w_qkv[...])
         dn_s[pl.ds(2 * c, 2)] = dn.reshape(2, 2, 64, width).astype(bf16)
         swap_dn(c).start()
@@ -336,56 +360,59 @@
                 d_s[2 * cols + lo : 2 * cols + hi, at] = dot_nt(d_oh, probs).astype(bf16)
 
     lax.fori_loop(0, 2, backward, 0)
-    columns(dy_s, dy_t)
-
-    def weight_grads(m):
-        m = (m + 2 * (1 - core)) % 4
-        at = pl.ds(pl.multiple_of(m * 16 * PAD, 16 * PAD), 16 * PAD)
-        to = pl.ds(m * 16, 16)
-        g[to, :, : 3 * cols] = (
-            dot_nt(n_t[at, :], d_s[...]).reshape(16, PAD, 3 * cols).astype(bf16)
-        )
-        g[to, :, 3 * cols :] = dot_nt(dy_t[at, :], o_s[...]).reshape(16, PAD, cols).astype(bf16)
-
-    def piece(c, a, h):
-        return g.at[pl.ds(((c * 4 + a) * 2 + h) * 4, 4)]
-
-    order = ((2, 0), (2, 1), (1, 1), (3, 0), (1, 0), (3, 1), (0, 0), (0, 1))
-    mine = [piece(core, (here + da) % 4, h) for da, h in order]
-    theirs = [piece(1 - core, (there + da) % 4, h) for da, h in order]
-    lax.fori_loop(0, 2, lambda m, _: (weight_grads(m), 0)[1], 0)
-    swaps = []
-    for i in range(8):
-        c = remote(theirs[i], sib.at[i], core_send.at[i], core_recv.at[i], sibling)
-        c.start()
-        swaps.append(c)
-    lax.fori_loop(2, 4, lambda m, _: (weight_grads(m), 0)[1], 0)
-
-    def fold(i):
-        swaps[i].wait_recv()
-        add_blocks(mine[i], (mine[i], sib.at[i]), 4)
+
+    def piece(a, h):
+        return g.at[pl.ds(((here + a) % 4 * 2 + h) * 4, 4)]
 
     copies = []
 
-    def send(src, dst, k, peer, sends, recvs):
+    def plan(src, dst, k, peer, sends, recvs):
         c = remote(src, dst, sends.at[k], recvs.at[k], peer)
-        c.start()
         copies.append(c)
         return c
 
+    def send(*what):
+        c = plan(*what)
+        c.start()
+        return c
+
     right, left = ring(True, 1), ring(True, -1)
-    fold(0)
-    c1r = send(mine[0], r1, 0, right, a_send, a_recv)
-    fold(1)
-    c1l = send(mine[1], l1, 1, left, a_send, a_recv)
-    fold(2)
-    c2r = send(mine[2], r2, 2, right, a_send, a_recv)
-    fold(3)
-    c2l = send(mine[3], l2, 3, left, a_send, a_recv)
-    fold(4)
-    fold(5)
-    fold(6)
-    fold(7)
+    c1r = plan(piece(2, 0), r1, 0, right, a_send, a_recv)
+    c1l = plan(piece(2, 1), l1, 1, left, a_send, a_recv)
+    c2r = plan(piece(1, 1), r2, 2, right, a_send, a_recv)
+    c2l = plan(piece(3, 0), l2, 3, left, a_send, a_recv)
+    for c in range(2):
+        swap_ntx(c).wait_recv()
+        swap_ox(c).wait_recv()
+        swap_dyx(c).wait_recv()
+        swap_dx(c).wait_recv()
+
+    def weight_grads(i, _):
+        a = (here + jnp.where(i < 2, 2 - i, 5 - i - (i // 3) * 2)) % 4
+        at = pl.ds(pl.multiple_of((core * 4 + a) * 8 * PAD, 8 * PAD), 8 * PAD)
+        at_x = pl.ds(pl.multiple_of(a * 8 * PAD, 8 * PAD), 8 * PAD)
+        to = pl.ds(a * 8, 8)
+        part = dot_nt(n_t[at, :], d_s[...]) + dot_nt(nt_x[at_x, :], d_x[...])
+        g[to, :, : 3 * cols] = part.reshape(8, PAD, 3 * cols).astype(bf16)
+        part = dot_nt(dy_t[at, :], o_s[...]) + dot_nt(dyt_x[at_x, :], o_x[...])
+        g[to, :, 3 * cols :] = part.reshape(8, PAD, cols).astype(bf16)
+
+        @pl.when(i == 0)
+        def _():
+            c1r.start()
+            c1l.start()
+
+        @pl.when(i == 1)
+        def _():
+            c2r.start()
+
+        @pl.when(i == 2)
+        def _():
+            c2l.start()
+
+        return 0
+
+    lax.fori_loop(0, 4, weight_grads, 0)
 
     drain_all(leave, r, all_send, all_recv, width + 128)
 
@@ -453,23 +480,22 @@
 
         lax.fori_loop(1, FRAME // 2, step, 0)
 
+    c1r.wait_recv()
+    add_blocks(piece(1, 0), (piece(1, 0), r1), 4)
+    c3r = send(piece(1, 0), r3, 4, right, a_send, a_recv)
+    c1l.wait_recv()
+    add_blocks(piece(3, 1), (piece(3, 1), l1), 4)
+    c3l = send(piece(3, 1), l3, 5, left, a_send, a_recv)
     home_each(lambda c: c.start(), home_local.start)
-
-    c1r.wait_recv()
-    add_blocks(mine[4], (mine[4], r1), 4)
-    c3r = send(mine[4], r3, 4, right, a_send, a_recv)
-    c1l.wait_recv()
-    add_blocks(mine[5], (mine[5], l1), 4)
-    c3l = send(mine[5], l3, 5, left, a_send, a_recv)
     c2l.wait_recv()
     c3r.wait_recv()
-    add_blocks(mine[6], (mine[6], r3, l2), 4)
+    add_blocks(piece(0, 0), (piece(0, 0), r3, l2), 4)
     c2r.wait_recv()
     c3l.wait_recv()
-    add_blocks(mine[7], (mine[7], r2, l3), 4)
+    add_blocks(piece(0, 1), (piece(0, 1), r2, l3), 4)
 
     right, left = ring(False, 1), ring(False, -1)
-    at = lambda h, d: g.at[((core * 4 + here) * 2 + h) * 4 + (there + d) % 4]
+    at = lambda h, d: g.at[(here * 2 + h) * 4 + (there + d) % 4]
     d1r = send(at(0, 2), br1, 0, right, b_send, b_recv)
     d1l = send(at(1, 2), bl1, 1, left, b_send, b_recv)
     d2r = send(at(1, 1), br2, 2, right, b_send, b_recv)
@@ -492,17 +518,27 @@
     e.wait_recv()
     out[...] = u[xh].astype(f32) + xr[...].astype(f32)
     home_each(lambda c: c.wait_recv(), home_local.wait)
+    for h in range(2):
+        t = iota((half, half), 0)
+        source = (t % 128 // 4) * 8 + (t % 4) * 2 + t // 128
+        pick = (iota((half, half), 1) == source).astype(bf16)
+        landed = d_recv[h * (FRAME // 2) : (h + 1) * (FRAME // 2)].reshape(half, width)
+        moved = dot(pick, landed).astype(bf16)
+        d_clip[h * 128 : (h + 1) * 128, :] = moved[:128]
+        d_clip[half + h * 128 : half + (h + 1) * 128, :] = moved[128:]
 
     e.wait_send()
     w_first.wait_send()
     w_second.wait_send()
-    for c in swaps:
-        c.wait_send()
     for c in copies:
         c.wait_send()
     for c in range(2):
         swap_o(c).wait_send()
         swap_dn(c).wait_send()
+        swap_ox(c).wait_send()
+        swap_ntx(c).wait_send()
+        swap_dyx(c).wait_send()
+        swap_dx(c).wait_send()
     home_each(lambda c: c.wait_send(), lambda: None)
 
 
@@ -523,11 +559,12 @@
         layer_kernel,
         out_shape=[
             jax.ShapeDtypeStruct((PAD, 4 * cols), f32),
-            jax.ShapeDtypeStruct((FRAME, each, width), bf16),
+            jax.ShapeDtypeStruct((tokens, width), bf16),
         ],
         in_specs=[anywhere, anywhere, vmem, anywhere, anywhere, anywhere],
         out_specs=[vmem, vmem],
         scratch_shapes=[
+            pltpu.VMEM((FRAME, each, width), bf16),
             wide,
             pltpu.VMEM((tokens, 128), bf16),
             carry,
@@ -551,8 +588,11 @@
             pltpu.VMEM((4, 64, width), bf16),
             pltpu.VMEM((FRAME * PAD, tokens), bf16),
             pltpu.VMEM((FRAME * PAD, tokens), bf16),
-            pltpu.VMEM((FRAME, PAD, 4 * cols), bf16),
-            pltpu.VMEM((8, 4, PAD, 4 * cols), bf16),
+            pltpu.VMEM((FRAME * PAD // 2, tokens), bf16),
+            pltpu.VMEM((FRAME * PAD // 2, tokens), bf16),
+            pltpu.VMEM((3 * cols, tokens), bf16),
+            narrow,
+            pltpu.VMEM((FRAME // 2, PAD, 4 * cols), bf16),
         ]
         + [piece] * 6
         + [block] * 8
@@ -561,7 +601,7 @@
             dma((5,)), dma, dma((2,)), dma((2,)),
             dma, dma((FRAME,)), dma((FRAME,)), dma, dma((FRAME,)), dma((FRAME,)),
             dma((2,)), dma((2,)), dma((2,)), dma((2,)),
-            dma((8,)), dma((8,)), dma((6,)), dma((6,)), dma((6,)), dma((6,)), dma, dma,
+            dma((2, 2)), dma((2, 2)), dma((2, 2)), dma((2, 2)), dma((6,)), dma((6,)), dma((6,)), dma((6,)), dma, dma,
         ],
         compiler_params=pltpu.CompilerParams(
             collective_id=0, has_side_effects=True, vmem_limit_bytes=VMEM_LIMIT
@@ -578,7 +618,7 @@
     ids = target_ids.reshape(tokens, 1)
     lane = iota((tokens, 128), 1)
     ids = jnp.where(lane == 0, ids // 32, jnp.where(lane == 1, ids % 32, 0)).astype(bf16)
-    reduced, returned = layer(
+    reduced, d_clip = layer(
         clip.reshape(tokens, width),
         ids,
         gain.reshape(1, width),
@@ -587,10 +627,6 @@
         old_table,
     )
 
-    t = iota((tokens, tokens), 0)
-    source = (t % patches // 4) * 8 + (t % 4) * 2 + t // patches
-    pick = iota((tokens, tokens), 1) == source
-    d_clip = dot(pick.astype(bf16), returned.reshape(tokens, width)).astype(bf16)
     reduced = reduced[:ROWS].reshape(ROWS, 4, cols)
     return (
         d_clip.reshape(frames_here, patches, width),

time: 139 us -> 135 us (0.971)
  the two profiles are of different devices: /device:TPU:0 before, /device:TPU:5 now
where the time goes in v5:
time: 135 us
  Pallas kernels  126 us (93%)
  local copies, waits for them, and re-layouts  7.16 us (5%)
    pallas_call x1, Pallas kernels, layer(): pl.pallas_call(layer_kernel, out_shape=[jax.ShapeDtypeStruct((PAD, 4 * co...  126 us
    unnamed x4, local copies, waits for them, and re-layouts  4.62 us

profile of v5, /device:TPU:5, one launch (start us, length us, event | category | flops | bytes accessed | tf_op | source)
XLA Modules:
  0.0 135.0 jit_solution(6379737590578046205)
XLA Ops:
  0.6 0.7 copy.13
  1.3 1.3 reshape.113.gain
  2.6 0.9 select_convert_fusion.ids
  3.5 126.3 %layer.1 = (f32[24,2816]{1,0:T(8,128)}, bf16[512,1408]{1,0:T(8,128)(2,1)}) custom-call(bf16[512,1408]{1,0:T(8,128)(2,1)} %bitcast.18, bf16[512,128]{1,0:T(8,128)(2,1)} %select_convert_fusion.ids, bf16[1,1408]{1,0:T(2,128)(2,1)} %reshape.113.gain, bf16[2112,1408]{1,0:T(8,128)(2,1)} %bitcast.17, bf16[704,1408]{1,0:T(8,128)(2,1)} %w_out_hbm.1, ...), custom_call_target="tpu_custom_call" | custom-call | tf_op jit(solution)/shard_map/layer/pallas_call | solution.py:558
  129.8 1.2 reshape.116
  130.9 0.1 slice.13
  131.0 0.6 copy.17
  131.7 0.7 copy.16
  132.4 2.6 %copy.19 = bf16[2,256,1408]{2,1,0:T(8,128)(2,1)} copy(bf16[2,256,1408]{2,1,0:T(8,128)(2,1)} %bitcast.19) | data formatting | bytes 2883584
  (2 shorter events, 0.0 us)

commit v6 on v5

--- a/solution.py
+++ b/solution.py
@@ -12,7 +12,6 @@
 VMEM_LIMIT = 63 * 2**20
 XH, Y, Z, CORE = 2, 4, 4, 2
 FRAME = XH * Y * Z * CORE
-CHAN = 2
 ROWS = 22
 PAD = 24
 
@@ -37,14 +36,9 @@
     return p, {"frame": p, "chan": (chan + far) % 2}
 
 
-def greet(k):
-    me = lax.axis_index("frame") * CHAN + lax.axis_index("chan")
-    other = (me + k) % (FRAME * CHAN)
+def greet(peer):
     pl.semaphore_signal(
-        pltpu.get_barrier_semaphore(),
-        inc=1,
-        device_id={"frame": other // CHAN, "chan": other % CHAN},
-        device_id_type=pl.DeviceIdType.MESH,
+        pltpu.get_barrier_semaphore(), inc=1, device_id=peer, device_id_type=pl.DeviceIdType.MESH
     )
 
 
@@ -132,11 +126,11 @@
 
 
 def layer_kernel(
-    clip, ids, gain, w_qkv_hbm, w_out_hbm, table_hbm, out, d_clip,
-    d_recv, x_v, ids_v, leave, r, w_qkv, w_out, w_other, table,
+    clip, ids, gain, w_qkv_hbm, w_out_hbm, table_hbm, out_qkv, out_o, d_clip,
+    d_recv, x_v, leave, r, w_qkv, w_out, w_other, table,
     x_s, ids_s, n_s, qkv_s, o_s, oo_s, p_s, dy_s, do_s, ds_s, d_s, dn_s, dno_s, n_t, dy_t,
     nt_x, dyt_x, d_x, o_x, g, r1, l1, r2, l2, r3, l3, br1, bl1, br2, bl2, br3, bl3, bmr, bml, u, xr,
-    load_sem, w_sem, w_send, w_recv, own_sem, all_send, all_recv, home_own, home_send, home_recv,
+    load_sem, w_sem, w_send, w_recv, own_sem, all_send, all_recv, home_own, home_send, home_recv, on_send, on_recv,
     o_send, o_recv, dn_send, dn_recv,
     ox_sems, ntx_sems, dyx_sems, dx_sems, a_send, a_recv, b_send, b_recv, x_send, x_recv,
 ):
@@ -170,43 +164,50 @@
 
     loads = [
         pltpu.make_async_copy(clip, x_v, load_sem.at[0]),
-        pltpu.make_async_copy(ids, ids_v, load_sem.at[1]),
-        pltpu.make_async_copy(w_out_hbm, w_out, load_sem.at[2]),
-        pltpu.make_async_copy(w_qkv_hbm, w_qkv, load_sem.at[3]),
-        pltpu.make_async_copy(table_hbm, table, load_sem.at[4]),
+        pltpu.make_async_copy(w_out_hbm, w_out, load_sem.at[1]),
+        pltpu.make_async_copy(w_qkv_hbm, w_qkv, load_sem.at[2]),
+        pltpu.make_async_copy(table_hbm, table, load_sem.at[3]),
     ]
     for c in loads:
         c.start()
     def greet_some(k, _):
-        greet(k)
-        return 0
-
-    lax.fori_loop(1, FRAME * CHAN, greet_some, 0)
+        greet(all_peer(k)[1])
+        return 0
+
+    lax.fori_loop(1, FRAME, greet_some, 0)
+    greet(partner)
+    greet(across)
 
     loads[0].wait()
-    loads[1].wait()
+    gain_row = gain[...].astype(f32).reshape(1, width)
+    id_row = jnp.concatenate([ids[0:1, :], ids[1:2, :]], axis=1).astype(f32)
 
     def leaving(j, _):
         t = iota((128, tokens), 0) + j * 128
         source = (t % 2) * half + (t // 8) * 4 + t % 8 // 2
-        pick = (iota((128, tokens), 1) == source).astype(bf16)
+        pick = iota((128, tokens), 1) == source
         to = pl.ds(j * 16, 16)
-        leave[to, :, :width] = dot(pick, x_v[...]).reshape(16, 8, width).astype(bf16)
-        leave[to, :, width:] = dot(pick, ids_v[...]).reshape(16, 8, 128).astype(bf16)
+        moved = dot(pick.astype(bf16), x_v[...])
+        leave[to, :, :width] = moved.reshape(16, 8, width).astype(bf16)
+        id_here = jnp.sum(jnp.where(pick, id_row, 0.0), axis=1, keepdims=True)
+        high = jnp.floor(id_here * (1.0 / 32.0))
+        lane = iota((128, 128), 1)
+        pair = jnp.where(lane == 0, high, jnp.where(lane == 1, id_here - high * 32.0, 0.0))
+        leave[to, :, width:] = pair.reshape(16, 8, 128).astype(bf16)
         return 0
 
     lax.fori_loop(0, 4, leaving, 0)
-    loads[2].wait()
-    pl.semaphore_wait(pltpu.get_barrier_semaphore(), FRAME * CHAN - 1)
+    loads[1].wait()
+    pl.semaphore_wait(pltpu.get_barrier_semaphore(), FRAME + 1)
 
     rows_half = cols // 2
     own_rows = pl.ds(pl.multiple_of(core * rows_half, 16), rows_half)
     w_first = remote(w_out.at[own_rows], w_other.at[own_rows], w_send.at[0], w_recv.at[0], partner)
+    start_all(leave, r, all_send, all_recv, own_sem, width + 128)
     w_first.start()
-    start_all(leave, r, all_send, all_recv, own_sem, width + 128)
     wait_all(leave, r, all_send, all_recv, own_sem, width + 128)
+    loads[2].wait()
     loads[3].wait()
-    loads[4].wait()
 
     def rows(c):
         return pl.ds(pl.multiple_of(c * half, half), half)
@@ -251,7 +252,7 @@
         x_s[rows(c), :] = x.astype(bf16)
         ids_s[rows(c), :] = moved[:, width:]
         xhat, _ = norm_terms(x)
-        normed = (xhat * gain[...].astype(f32)).astype(bf16)
+        normed = (xhat * gain_row).astype(bf16)
         n_s[rows(c), :] = normed
         for i in range(3):
             qkv = dot_nt(w_qkv[i * cols : (i + 1) * cols, :], normed)
@@ -424,7 +425,7 @@
         at = pl.ds(pl.multiple_of(p * 128 + kept * 64, 64), 64)
         dn = dn_s[p, kept].astype(f32) + dno_s[p].astype(f32)
         xhat, rstd = norm_terms(x_s[at, :].astype(f32))
-        gs = dn * gain[...].astype(f32)
+        gs = dn * gain_row
         back = rstd * (
             gs
             - jnp.mean(gs, axis=-1, keepdims=True)
@@ -449,18 +450,18 @@
     lax.fori_loop(0, 2, to_home, 0)
 
     f = lax.axis_index("frame")
-    own = (kept + xh) % 2 == 0
-
-    def home_copy(k, c):
-        q = (f + k) % (FRAME // 2)
-        return pltpu.make_async_remote_copy(
-            src_ref=part(leave, q, width), dst_ref=d_recv.at[f],
-            send_sem=home_send.at[2 * k + c], recv_sem=home_recv.at[2 * k + c],
-            device_id={"frame": kept * (FRAME // 2) + q, "chan": (chan + c) % 2},
-            device_id_type=pl.DeviceIdType.MESH,
+    spots = FRAME // 2
+    spot = f % spots
+    own = core == chan
+
+    def home_copy(k):
+        q = (spot + k) % spots
+        return remote(
+            part(leave, q, width), d_recv.at[f], home_send.at[k], home_recv.at[f // 2],
+            {"frame": kept * spots + q, "chan": core},
         )
 
-    home_local = pltpu.make_async_copy(part(leave, f % (FRAME // 2), width), d_recv.at[f], home_own)
+    home_local = pltpu.make_async_copy(part(leave, spot, width), d_recv.at[f], home_own)
 
     def home_each(run, run_own):
         @pl.when(own)
@@ -469,24 +470,52 @@
 
         @pl.when(jnp.logical_not(own))
         def _():
-            run(home_copy(0, 0))
-
-        run(home_copy(0, 1))
+            run(home_copy(0))
 
         def step(k, _):
-            run(home_copy(k, 0))
-            run(home_copy(k, 1))
+            run(home_copy(k))
             return 0
 
-        lax.fori_loop(1, FRAME // 2, step, 0)
-
+        lax.fori_loop(1, spots, step, 0)
+
+    def pass_on(i):
+        return remote(d_recv.at[i], d_recv.at[i], on_send.at[i // 2], on_recv.at[i // 2], partner)
+
+    def landed(k, _):
+        k = 2 * k + (core + chan) % 2
+        for n in range(2):
+            source = n * spots + (spot - k + spots) % spots
+            local = jnp.logical_and(source == f, own)
+
+            @pl.when(local)
+            def _():
+                home_local.wait()
+
+            @pl.when(jnp.logical_not(local))
+            def _(source=source):
+                remote(
+                    part(leave, 0, width), d_recv.at[source], home_send.at[0],
+                    home_recv.at[source // 2], partner,
+                ).wait_recv()
+
+            pass_on(source).start()
+        return 0
+
+    def passed_on(run):
+        def step(i, _):
+            run(i)
+            return 0
+
+        lax.fori_loop(0, spots, step, 0)
+
+    home_each(lambda c: c.start(), home_local.start)
     c1r.wait_recv()
     add_blocks(piece(1, 0), (piece(1, 0), r1), 4)
     c3r = send(piece(1, 0), r3, 4, right, a_send, a_recv)
     c1l.wait_recv()
     add_blocks(piece(3, 1), (piece(3, 1), l1), 4)
     c3l = send(piece(3, 1), l3, 5, left, a_send, a_recv)
-    home_each(lambda c: c.start(), home_local.start)
+    lax.fori_loop(0, spots // 2, landed, 0)
     c2l.wait_recv()
     c3r.wait_recv()
     add_blocks(piece(0, 0), (piece(0, 0), r3, l2), 4)
@@ -516,8 +545,11 @@
     e = remote(u.at[1 - xh], xr, x_send, x_recv, across)
     e.start()
     e.wait_recv()
-    out[...] = u[xh].astype(f32) + xr[...].astype(f32)
-    home_each(lambda c: c.wait_recv(), home_local.wait)
+    total = u[xh].astype(f32) + xr[...].astype(f32)
+    for i in range(3):
+        out_qkv[i] = total[:ROWS, i * cols : (i + 1) * cols]
+    out_o[...] = total[:ROWS, 3 * cols :]
+    passed_on(lambda i: pass_on(2 * i + 1 - chan).wait_recv())
     for h in range(2):
         t = iota((half, half), 0)
         source = (t % 128 // 4) * 8 + (t % 4) * 2 + t // 128
@@ -540,6 +572,7 @@
         swap_dyx(c).wait_send()
         swap_dx(c).wait_send()
     home_each(lambda c: c.wait_send(), lambda: None)
+    passed_on(lambda i: pass_on(2 * i + chan).wait_send())
 
 
 def layer(clip, ids, gain, w_qkv, w_out, table):
@@ -558,15 +591,15 @@
     return pl.pallas_call(
         layer_kernel,
         out_shape=[
-            jax.ShapeDtypeStruct((PAD, 4 * cols), f32),
+            jax.ShapeDtypeStruct((3, ROWS, cols), f32),
+            jax.ShapeDtypeStruct((ROWS, cols), f32),
             jax.ShapeDtypeStruct((tokens, width), bf16),
         ],
-        in_specs=[anywhere, anywhere, vmem, anywhere, anywhere, anywhere],
-        out_specs=[vmem, vmem],
+        in_specs=[anywhere, vmem, vmem, anywhere, anywhere, anywhere],
+        out_specs=[vmem, vmem, vmem],
         scratch_shapes=[
             pltpu.VMEM((FRAME, each, width), bf16),
             wide,
-            pltpu.VMEM((tokens, 128), bf16),
             carry,
             carry,
             pltpu.VMEM((3 * cols, width), bf16),
@@ -598,8 +631,9 @@
         + [block] * 8
         + [pltpu.VMEM((2, PAD, 4 * cols), bf16), block]
         + [
-            dma((5,)), dma, dma((2,)), dma((2,)),
-            dma, dma((FRAME,)), dma((FRAME,)), dma, dma((FRAME,)), dma((FRAME,)),
+            dma((4,)), dma, dma((2,)), dma((2,)),
+            dma, dma((FRAME,)), dma((FRAME,)),
+            dma, dma((FRAME // 2,)), dma((FRAME // 2,)), dma((FRAME // 2,)), dma((FRAME // 2,)),
             dma((2,)), dma((2,)), dma((2,)), dma((2,)),
             dma((2, 2)), dma((2, 2)), dma((2, 2)), dma((2, 2)), dma((6,)), dma((6,)), dma((6,)), dma((6,)), dma, dma,
         ],
@@ -615,24 +649,15 @@
     cols = w_qkv.shape[2]
     tokens = frames_here * patches
 
-    ids = target_ids.reshape(tokens, 1)
-    lane = iota((tokens, 128), 1)
-    ids = jnp.where(lane == 0, ids // 32, jnp.where(lane == 1, ids % 32, 0)).astype(bf16)
-    reduced, d_clip = layer(
+    d_qkv, d_out, d_clip = layer(
         clip.reshape(tokens, width),
-        ids,
-        gain.reshape(1, width),
+        target_ids,
+        gain,
         w_qkv.transpose(0, 2, 1).reshape(3 * cols, width),
         w_out,
         old_table,
     )
-
-    reduced = reduced[:ROWS].reshape(ROWS, 4, cols)
-    return (
-        d_clip.reshape(frames_here, patches, width),
-        reduced[:, :3].transpose(1, 0, 2),
-        reduced[:, 3].T,
-    )
+    return d_clip.reshape(frames_here, patches, width), d_qkv, d_out.T
 
 
 def solution(mesh):

time: 135 us -> 121 us (0.90)
  the two profiles are of different devices: /device:TPU:5 before, /device:TPU:0 now
where the time goes in v6:
time: 121 us; the launch traced here: 120 us
  Pallas kernels  116 us (96%)
  local copies, waits for them, and re-layouts  3.94 us (3%)
    pallas_call x1, Pallas kernels, layer(): pl.pallas_call(layer_kernel, out_shape=[jax.ShapeDtypeStruct((3, ROWS, co...  116 us
    unnamed x7, local copies, waits for them, and re-layouts  3.94 us

profile of v6, /device:TPU:0, one launch (start us, length us, event | category | flops | bytes accessed | tf_op | source)
XLA Modules:
  0.0 120.2 jit_solution(9478076061686246913)
XLA Ops:
  0.6 115.6 %layer.1 = (f32[3,22,704]{2,1,0:T(8,128)}, f32[22,704]{1,0:T(8,128)}, bf16[512,1408]{1,0:T(8,128)(2,1)}) custom-call(bf16[512,1408]{1,0:T(8,128)(2,1)} %bitcast.7, s32[2,256]{1,0:T(2,128)} %ids.1, bf16[1408]{0:T(1024)(128)(2,1)} %gain.1, bf16[2112,1408]{1,0:T(8,128)(2,1)} %bitcast.6, bf16[704,1408]{1,0:T(8,128)(2,1)} %w_out_hbm.1, bf16[1024,1408]{1,0:T(8,128)(2,1)} %table_hbm.1), custom_call_target="tpu_custom_call" | custom-call | tf_op jit(solution)/shard_map/layer/pallas_call | solution.py:591
  116.2 0.0 copy-start
  116.2 0.0 copy-start.1
  116.2 2.6 %copy.12 = bf16[2,256,1408]{2,1,0:T(8,128)(2,1)} copy(bf16[2,256,1408]{2,1,0:T(8,128)(2,1)} %bitcast.8) | data formatting | bytes 2883584
  118.9 0.0 copy-done
  118.9 0.7 copy.13
  119.5 0.0 copy-done.1
  119.5 0.6 copy.14
Async XLA Ops:
  116.2 2.6 %copy-start = (f32[3,22,704]{2,1,0:T(8,128)S(1)}, f32[3,22,704]{2,1,0:T(8,128)}, u32[]{:S(2)}) copy-start(f32[3,22,704]{2,1,0:T(8,128)} %get-tuple-element.13) | copy-start | bytes 557572
  116.2 3.3 %copy-start.1 = (f32[22,704]{1,0:T(8,128)S(1)}, f32[22,704]{1,0:T(8,128)}, u32[]{:S(2)}) copy-start(f32[22,704]{1,0:T(8,128)} %get-tuple-element.8) | copy-start | bytes 185860

commit v7 on v6

--- a/solution.py
+++ b/solution.py
@@ -55,16 +55,6 @@
     )
 
 
-def start_all(src, dst, sends, recvs, own_sem, width):
-    def start(k, _):
-        all_copy(src, dst, sends, recvs, k, width).start()
-        return 0
-
-    lax.fori_loop(1, FRAME, start, 0)
-    f = lax.axis_index("frame")
-    pltpu.make_async_copy(part(src, f, width), part(dst, f, width), own_sem).start()
-
-
 def wait_all(src, dst, sends, recvs, own_sem, width):
     f = lax.axis_index("frame")
     pltpu.make_async_copy(part(src, f, width), part(dst, f, width), own_sem).wait()
@@ -126,8 +116,8 @@
 
 
 def layer_kernel(
-    clip, ids, gain, w_qkv_hbm, w_out_hbm, table_hbm, out_qkv, out_o, d_clip,
-    d_recv, x_v, leave, r, w_qkv, w_out, w_other, table,
+    clip, ids, gain, w_qkv_hbm, w_out_hbm, table_hbm, out, d_recv,
+    x_v, leave, r, w_qkv, w_out, w_other, table,
     x_s, ids_s, n_s, qkv_s, o_s, oo_s, p_s, dy_s, do_s, ds_s, d_s, dn_s, dno_s, n_t, dy_t,
     nt_x, dyt_x, d_x, o_x, g, r1, l1, r2, l2, r3, l3, br1, bl1, br2, bl2, br3, bl3, bmr, bml, u, xr,
     load_sem, w_sem, w_send, w_recv, own_sem, all_send, all_recv, home_own, home_send, home_recv, on_send, on_recv,
@@ -182,7 +172,10 @@
     gain_row = gain[...].astype(f32).reshape(1, width)
     id_row = jnp.concatenate([ids[0:1, :], ids[1:2, :]], axis=1).astype(f32)
 
-    def leaving(j, _):
+    me = lax.axis_index("frame")
+
+    def leaving(i, _):
+        j = (me // 16 + i) % 4
         t = iota((128, tokens), 0) + j * 128
         source = (t % 2) * half + (t // 8) * 4 + t % 8 // 2
         pick = iota((128, tokens), 1) == source
@@ -194,16 +187,33 @@
         lane = iota((128, 128), 1)
         pair = jnp.where(lane == 0, high, jnp.where(lane == 1, id_here - high * 32.0, 0.0))
         leave[to, :, width:] = pair.reshape(16, 8, 128).astype(bf16)
-        return 0
-
+
+        def start(d, _):
+            p = j * 16 + (me + d) % 16
+            k = (p - me + FRAME) % FRAME
+
+            @pl.when(k != 0)
+            def _():
+                all_copy(leave, r, all_send, all_recv, k, width + 128).start()
+
+            @pl.when(k == 0)
+            def _():
+                pltpu.make_async_copy(
+                    part(leave, me, width + 128), part(r, me, width + 128), own_sem
+                ).start()
+
+            return 0
+
+        lax.fori_loop(0, 16, start, 0)
+        return 0
+
+    pl.semaphore_wait(pltpu.get_barrier_semaphore(), FRAME + 1)
     lax.fori_loop(0, 4, leaving, 0)
     loads[1].wait()
-    pl.semaphore_wait(pltpu.get_barrier_semaphore(), FRAME + 1)
 
     rows_half = cols // 2
     own_rows = pl.ds(pl.multiple_of(core * rows_half, 16), rows_half)
     w_first = remote(w_out.at[own_rows], w_other.at[own_rows], w_send.at[0], w_recv.at[0], partner)
-    start_all(leave, r, all_send, all_recv, own_sem, width + 128)
     w_first.start()
     wait_all(leave, r, all_send, all_recv, own_sem, width + 128)
     loads[2].wait()
@@ -515,7 +525,7 @@
     c1l.wait_recv()
     add_blocks(piece(3, 1), (piece(3, 1), l1), 4)
     c3l = send(piece(3, 1), l3, 5, left, a_send, a_recv)
-    lax.fori_loop(0, spots // 2, landed, 0)
+    lax.fori_loop(0, 8, landed, 0)
     c2l.wait_recv()
     c3r.wait_recv()
     add_blocks(piece(0, 0), (piece(0, 0), r3, l2), 4)
@@ -529,6 +539,7 @@
     d1l = send(at(1, 2), bl1, 1, left, b_send, b_recv)
     d2r = send(at(1, 1), br2, 2, right, b_send, b_recv)
     d2l = send(at(0, 3), bl2, 3, left, b_send, b_recv)
+    lax.fori_loop(8, spots // 2, landed, 0)
     d1r.wait_recv()
     bmr[...] = (at(0, 1)[...].astype(f32) + br1[...].astype(f32)).astype(bf16)
     d3r = send(bmr, br3, 4, right, b_send, b_recv)
@@ -545,19 +556,8 @@
     e = remote(u.at[1 - xh], xr, x_send, x_recv, across)
     e.start()
     e.wait_recv()
-    total = u[xh].astype(f32) + xr[...].astype(f32)
-    for i in range(3):
-        out_qkv[i] = total[:ROWS, i * cols : (i + 1) * cols]
-    out_o[...] = total[:ROWS, 3 * cols :]
+    out[...] = u[xh].astype(f32) + xr[...].astype(f32)
     passed_on(lambda i: pass_on(2 * i + 1 - chan).wait_recv())
-    for h in range(2):
-        t = iota((half, half), 0)
-        source = (t % 128 // 4) * 8 + (t % 4) * 2 + t // 128
-        pick = (iota((half, half), 1) == source).astype(bf16)
-        landed = d_recv[h * (FRAME // 2) : (h + 1) * (FRAME // 2)].reshape(half, width)
-        moved = dot(pick, landed).astype(bf16)
-        d_clip[h * 128 : (h + 1) * 128, :] = moved[:128]
-        d_clip[half + h * 128 : half + (h + 1) * 128, :] = moved[128:]
 
     e.wait_send()
     w_first.wait_send()
@@ -591,14 +591,12 @@
     return pl.pallas_call(
         layer_kernel,
         out_shape=[
-            jax.ShapeDtypeStruct((3, ROWS, cols), f32),
-            jax.ShapeDtypeStruct((ROWS, cols), f32),
-            jax.ShapeDtypeStruct((tokens, width), bf16),
+            jax.ShapeDtypeStruct((PAD, 4 * cols), f32),
+            jax.ShapeDtypeStruct((FRAME, each, width), bf16),
         ],
         in_specs=[anywhere, vmem, vmem, anywhere, anywhere, anywhere],
-        out_specs=[vmem, vmem, vmem],
+        out_specs=[vmem, vmem],
         scratch_shapes=[
-            pltpu.VMEM((FRAME, each, width), bf16),
             wide,
             carry,
             carry,
@@ -644,12 +642,45 @@
     )(clip, ids, gain, w_qkv, w_out, table)
 
 
+def settle_kernel(total, d_recv, d_qkv, d_out, d_clip):
+    cols = d_out.shape[1]
+    half, width = d_clip.shape[0] // 2, d_clip.shape[1]
+    for i in range(3):
+        d_qkv[i] = total[:ROWS, i * cols : (i + 1) * cols]
+    d_out[...] = total[:ROWS, 3 * cols :]
+    for h in range(2):
+        t = iota((half, half), 0)
+        source = (t % 128 // 4) * 8 + (t % 4) * 2 + t // 128
+        pick = (iota((half, half), 1) == source).astype(bf16)
+        landed = d_recv[h * (FRAME // 2) : (h + 1) * (FRAME // 2)].reshape(half, width)
+        moved = dot(pick, landed).astype(bf16)
+        d_clip[h * 128 : (h + 1) * 128, :] = moved[:128]
+        d_clip[half + h * 128 : half + (h + 1) * 128, :] = moved[128:]
+
+
+def settle(total, d_recv):
+    cols = total.shape[1] // 4
+    vmem = pl.BlockSpec(memory_space=pltpu.VMEM)
+    return pl.pallas_call(
+        settle_kernel,
+        out_shape=[
+            jax.ShapeDtypeStruct((3, ROWS, cols), f32),
+            jax.ShapeDtypeStruct((ROWS, cols), f32),
+            jax.ShapeDtypeStruct((d_recv.shape[0] * d_recv.shape[1], d_recv.shape[2]), bf16),
+        ],
+        in_specs=[vmem, vmem],
+        out_specs=[vmem, vmem, vmem],
+        compiler_params=pltpu.CompilerParams(vmem_limit_bytes=32 * 2**20),
+        name="settle",
+    )(total, d_recv)
+
+
 def body(clip, gain, w_qkv, w_out, old_table, target_ids):
     frames_here, patches, width = clip.shape
     cols = w_qkv.shape[2]
     tokens = frames_here * patches
 
-    d_qkv, d_out, d_clip = layer(
+    total, d_recv = layer(
         clip.reshape(tokens, width),
         target_ids,
         gain,
@@ -657,6 +688,7 @@
         w_out,
         old_table,
     )
+    d_qkv, d_out, d_clip = settle(total, d_recv)
     return d_clip.reshape(frames_here, patches, width), d_qkv, d_out.T
 
 

time: 121 us -> 118 us (0.975)
  Pallas kernels: 116 us -> 114 us
  local copies, waits for them, and re-layouts: 3.94 us -> 2.31 us
    unnamed x7 -> x4, local copies, waits for them, and re-layouts: 3.94 us -> 2.31 us
    pallas_call x1 -> x2, Pallas kernels: 116 us -> 114 us  [the longest x1 112 us: layer(): pl.pallas_call(layer_kernel, out_shape=[jax.ShapeDtypeStruct((PAD, 4 * co...]
where the time goes in v7:
time: 118 us; the launch traced here: 117 us
  Pallas kernels  114 us (97%)
  local copies, waits for them, and re-layouts  2.31 us (2%)
    pallas_call x1, Pallas kernels, layer(): pl.pallas_call(layer_kernel, out_shape=[jax.ShapeDtypeStruct((PAD, 4 * co...  112 us

profile of v7, /device:TPU:0, one launch (start us, length us, event | category | flops | bytes accessed | tf_op | source)
XLA Modules:
  0.0 117.1 jit_solution(11348665416670369117)
XLA Ops:
  0.6 112.5 %layer.1 = (f32[24,2816]{1,0:T(8,128)}, bf16[64,8,1408]{2,1,0:T(8,128)(2,1)}) custom-call(bf16[512,1408]{1,0:T(8,128)(2,1)} %bitcast.7, s32[2,256]{1,0:T(2,128)} %ids.1, bf16[1408]{0:T(1024)(128)(2,1)} %gain.1, bf16[2112,1408]{1,0:T(8,128)(2,1)} %bitcast.6, bf16[704,1408]{1,0:T(8,128)(2,1)} %w_out_hbm.1, bf16[1024,1408]{1,0:T(8,128)(2,1)} %table_hbm.1), custom_call_target="tpu_custom_call" | custom-call | tf_op jit(solution)/shard_map/layer/pallas_call | solution.py:591
  113.1 0.0 copy-start
  113.1 1.4 %copy-done = bf16[64,8,1408]{2,1,0:T(8,128)(2,1)S(1)} copy-done((bf16[64,8,1408]{2,1,0:T(8,128)(2,1)S(1)}, bf16[64,8,1408]{2,1,0:T(8,128)(2,1)}, u32[]{:S(2)}) %copy-start) | copy-done | bytes 1441816
  114.5 0.0 copy-start.1
  114.5 1.0 copy-done.1
  115.4 1.7 %settle.1 = (f32[3,22,704]{2,1,0:T(8,128)}, f32[22,704]{1,0:T(8,128)}, bf16[512,1408]{1,0:T(8,128)(2,1)}) custom-call(f32[24,2816]{1,0:T(8,128)S(1)} %copy-done.1, bf16[64,8,1408]{2,1,0:T(8,128)(2,1)S(1)} %copy-done), custom_call_target="tpu_custom_call" | custom-call | tf_op jit(solution)/shard_map/settle/pallas_call | solution.py:664
Async XLA Ops:
  113.1 1.4 %copy-start = (bf16[64,8,1408]{2,1,0:T(8,128)(2,1)S(1)}, bf16[64,8,1408]{2,1,0:T(8,128)(2,1)}, u32[]{:S(2)}) copy-start(bf16[64,8,1408]{2,1,0:T(8,128)(2,1)} %get-tuple-element.9.d_recv) | copy-start | bytes 4325380
  114.5 1.0 copy-start.1

commit v8 on v7

--- a/solution.py
+++ b/solution.py
@@ -326,13 +326,13 @@
     lax.fori_loop(0, 2, targets, 0)
     w_second.wait_recv()
 
+    drain_all(leave, r, all_send, all_recv, width + 128)
+
     def backward(c, _):
         swap_o(c).wait_recv()
         branch = dot_tn(o_s[:, rows(c)], w_out[...]) + dot_tn(oo_s[:, rows(c)], w_other[...])
         d_y = (x_s[rows(c), :].astype(f32) + branch - x_v[rows(c), :].astype(f32)).astype(bf16)
         dy_s[rows(c), :] = d_y
-        alone(functools.partial(columns, dy_s, dy_t, c))
-        swap_dyx(c).start()
         d_o = dot_nt(w_out[...], d_y)
         for h in range(n_heads):
             do_s[h] = d_o[h * HEAD_DIM : (h + 1) * HEAD_DIM].astype(bf16)
@@ -342,6 +342,8 @@
         dn = dot_tn(d_s[:, rows(c)], w_qkv[...])
         dn_s[pl.ds(2 * c, 2)] = dn.reshape(2, 2, 64, width).astype(bf16)
         swap_dn(c).start()
+        alone(functools.partial(columns, dy_s, dy_t, c))
+        swap_dyx(c).start()
         return 0
 
     def score_heads(c):
@@ -395,7 +397,6 @@
     for c in range(2):
         swap_ntx(c).wait_recv()
         swap_ox(c).wait_recv()
-        swap_dyx(c).wait_recv()
         swap_dx(c).wait_recv()
 
     def weight_grads(i, _):
@@ -405,6 +406,12 @@
         to = pl.ds(a * 8, 8)
         part = dot_nt(n_t[at, :], d_s[...]) + dot_nt(nt_x[at_x, :], d_x[...])
         g[to, :, : 3 * cols] = part.reshape(8, PAD, 3 * cols).astype(bf16)
+
+        @pl.when(i == 0)
+        def _():
+            swap_dyx(0).wait_recv()
+            swap_dyx(1).wait_recv()
+
         part = dot_nt(dy_t[at, :], o_s[...]) + dot_nt(dyt_x[at_x, :], o_x[...])
         g[to, :, 3 * cols :] = part.reshape(8, PAD, cols).astype(bf16)
 
@@ -424,8 +431,6 @@
         return 0
 
     lax.fori_loop(0, 4, weight_grads, 0)
-
-    drain_all(leave, r, all_send, all_recv, width + 128)
 
     def finish(p, _):
         @pl.when(p % 2 == 0)
@@ -525,7 +530,7 @@
     c1l.wait_recv()
     add_blocks(piece(3, 1), (piece(3, 1), l1), 4)
     c3l = send(piece(3, 1), l3, 5, left, a_send, a_recv)
-    lax.fori_loop(0, 8, landed, 0)
+    lax.fori_loop(0, 12, landed, 0)
     c2l.wait_recv()
     c3r.wait_recv()
     add_blocks(piece(0, 0), (piece(0, 0), r3, l2), 4)
@@ -539,7 +544,7 @@
     d1l = send(at(1, 2), bl1, 1, left, b_send, b_recv)
     d2r = send(at(1, 1), br2, 2, right, b_send, b_recv)
     d2l = send(at(0, 3), bl2, 3, left, b_send, b_recv)
-    lax.fori_loop(8, spots // 2, landed, 0)
+    lax.fori_loop(12, spots // 2, landed, 0)
     d1r.wait_recv()
     bmr[...] = (at(0, 1)[...].astype(f32) + br1[...].astype(f32)).astype(bf16)
     d3r = send(bmr, br3, 4, right, b_send, b_recv)
@@ -644,32 +649,42 @@
 
 def settle_kernel(total, d_recv, d_qkv, d_out, d_clip):
     cols = d_out.shape[1]
-    half, width = d_clip.shape[0] // 2, d_clip.shape[1]
-    for i in range(3):
-        d_qkv[i] = total[:ROWS, i * cols : (i + 1) * cols]
-    d_out[...] = total[:ROWS, 3 * cols :]
-    for h in range(2):
-        t = iota((half, half), 0)
-        source = (t % 128 // 4) * 8 + (t % 4) * 2 + t // 128
-        pick = (iota((half, half), 1) == source).astype(bf16)
-        landed = d_recv[h * (FRAME // 2) : (h + 1) * (FRAME // 2)].reshape(half, width)
-        moved = dot(pick, landed).astype(bf16)
-        d_clip[h * 128 : (h + 1) * 128, :] = moved[:128]
-        d_clip[half + h * 128 : half + (h + 1) * 128, :] = moved[128:]
+    width = d_clip.shape[2]
+    half = 2 * d_clip.shape[1]
+
+    @pl.when(pl.program_id(0) == 0)
+    def _():
+        for i in range(3):
+            d_qkv[i] = total[:ROWS, i * cols : (i + 1) * cols]
+        d_out[...] = total[:ROWS, 3 * cols :]
+
+    t = iota((half, half), 0)
+    source = (t % 128 // 4) * 8 + (t % 4) * 2 + t // 128
+    pick = (iota((half, half), 1) == source).astype(bf16)
+    moved = dot(pick, d_recv[...].reshape(half, width))
+    d_clip[...] = moved.reshape(2, 128, width).astype(bf16)
 
 
 def settle(total, d_recv):
     cols = total.shape[1] // 4
-    vmem = pl.BlockSpec(memory_space=pltpu.VMEM)
+    sources, each, width = d_recv.shape
     return pl.pallas_call(
         settle_kernel,
+        grid=(2,),
         out_shape=[
             jax.ShapeDtypeStruct((3, ROWS, cols), f32),
             jax.ShapeDtypeStruct((ROWS, cols), f32),
-            jax.ShapeDtypeStruct((d_recv.shape[0] * d_recv.shape[1], d_recv.shape[2]), bf16),
+            jax.ShapeDtypeStruct((2, sources * each // 2, width), bf16),
         ],
-        in_specs=[vmem, vmem],
-        out_specs=[vmem, vmem, vmem],
+        in_specs=[
+            pl.BlockSpec((PAD, 4 * cols), lambda h: (0, 0)),
+            pl.BlockSpec((sources // 2, each, width), lambda h: (h, 0, 0)),
+        ],
+        out_specs=[
+            pl.BlockSpec((3, ROWS, cols), lambda h: (0, 0, 0)),
+            pl.BlockSpec((ROWS, cols), lambda h: (0, 0)),
+            pl.BlockSpec((2, sources * each // 4, width), lambda h: (0, h, 0)),
+        ],
         compiler_params=pltpu.CompilerParams(vmem_limit_bytes=32 * 2**20),
         name="settle",
     )(total, d_recv)
@@ -689,7 +704,7 @@
         old_table,
     )
     d_qkv, d_out, d_clip = settle(total, d_recv)
-    return d_clip.reshape(frames_here, patches, width), d_qkv, d_out.T
+    return d_clip, d_qkv, d_out.T
 
 
 def solution(mesh):

time: 118 us -> 117 us (level)
  no operation moved by 1% of the time
where the time goes in v8:
time: 117 us
  Pallas kernels  114 us (97%)
  local copies, waits for them, and re-layouts  2.31 us (2%)
    pallas_call x1, Pallas kernels, layer(): pl.pallas_call(layer_kernel, out_shape=[jax.ShapeDtypeStruct((PAD, 4 * co...  112 us

profile of v8, /device:TPU:0, one launch (start us, length us, event | category | flops | bytes accessed | tf_op | source)
XLA Modules:
  0.0 117.1 jit_solution(5781562721227223392)
XLA Ops:
  0.6 112.4 %layer.1 = (f32[24,2816]{1,0:T(8,128)}, bf16[64,8,1408]{2,1,0:T(8,128)(2,1)}) custom-call(bf16[512,1408]{1,0:T(8,128)(2,1)} %bitcast.6, s32[2,256]{1,0:T(2,128)} %ids.1, bf16[1408]{0:T(1024)(128)(2,1)} %gain.1, bf16[2112,1408]{1,0:T(8,128)(2,1)} %bitcast.5, bf16[704,1408]{1,0:T(8,128)(2,1)} %w_out_hbm.1, bf16[1024,1408]{1,0:T(8,128)(2,1)} %table_hbm.1), custom_call_target="tpu_custom_call" | custom-call | tf_op jit(solution)/shard_map/layer/pallas_call | solution.py:596
  113.0 0.0 copy-start
  113.0 1.4 %copy-done = bf16[64,8,1408]{2,1,0:T(8,128)(2,1)S(1)} copy-done((bf16[64,8,1408]{2,1,0:T(8,128)(2,1)S(1)}, bf16[64,8,1408]{2,1,0:T(8,128)(2,1)}, u32[]{:S(2)}) %copy-start) | copy-done | bytes 1441816
  114.4 0.0 copy-start.1
  114.4 1.0 copy-done.1
  115.3 1.7 %settle.1 = (f32[3,22,704]{2,1,0:T(8,128)}, f32[22,704]{1,0:T(8,128)}, bf16[2,256,1408]{2,1,0:T(8,128)(2,1)}) custom-call(f32[24,2816]{1,0:T(8,128)S(1)} %copy-done.1, bf16[64,8,1408]{2,1,0:T(8,128)(2,1)S(1)} %copy-done), custom_call_target="tpu_custom_call" | custom-call | tf_op jit(solution)/shard_map/settle/pallas_call | solution.py:671
Async XLA Ops:
  113.0 1.4 %copy-start = (bf16[64,8,1408]{2,1,0:T(8,128)(2,1)S(1)}, bf16[64,8,1408]{2,1,0:T(8,128)(2,1)}, u32[]{:S(2)}) copy-start(bf16[64,8,1408]{2,1,0:T(8,128)(2,1)} %get-tuple-element.9.d_recv) | copy-start | bytes 4325380
  114.4 1.0 copy-start.1
